TPU v7x, 32 devices: a whole 2x2x4 slice. The times are simulated.
32 devices in a mesh: cell: 8 (over z, y), dp: 4 (over x, core).
Axes of the slice: x: 2, y: 2, z: 4, core: 2. Of those that a mesh axis runs over, the one named last changes fastest.
Arguments:
- state: bfloat16 [163840, 128], P(('cell', 'dp')), may hold values from -6 to 6
- cell_coordinate: bfloat16 [3, 163840], P(None, ('cell', 'dp')), may hold values from 0 to 1
- member_predictions: bfloat16 [4, 1024, 128], P('dp', 'cell'), may hold values from -6 to 6
- measured_values: float32 [4, 1024], P('dp', 'cell'), may hold values from -64 to 64
- obs_error_variance: float32 [4, 1024], P('dp', 'cell'), may hold values from 4 to 64
- observation_coordinate: bfloat16 [4, 3, 1024], P('dp', None, 'cell'), may hold values from 0 to 1
- localization_tile_pairs: int32 [32, 4, 2, 256], P(('cell', 'dp')), may hold values from 0 to 39, as said below
- used_pair_count: int32 [32, 4], P(('cell', 'dp')), may hold values from 1 to 256, as said below
Outputs:
- analysis: bfloat16 [163840, 128], P(('cell', 'dp'))
Inputs may be any that keep to these rules, and one draw needn't show every extreme that they name: `localization_tile_pairs`: row 0 names a cell tile of the block (below 40), row 1 an observation tile of the batch (below 8); only the first used_pair_count entries count, and a pair may repeat. `used_pair_count`: in every batch some blocks list exactly 256 pairs.
All inputs are finite; a program needn't handle non-finite values.
Results may differ from a plain program's by a relative error of at most 0.011.
Values may be sent and summed in bfloat16 or wider, within the bound.
No kernel may reach another device: no remote copies, remote signals or barrier semaphores. Data moves between devices by JAX's collectives and lax.ppermute only.
A program may use at most 192 MiB of HBM per device.

v0:
```python
import functools
import math

import jax
import jax.numpy as jnp
from jax import lax
from jax.experimental import pallas as pl
from jax.experimental.pallas import tpu as pltpu
from jax.sharding import PartitionSpec as P

CT = 128
OBS_DEV = 128
EXTRA = 16
taper_rate = 2.0
LOG2E = math.log2(math.e)
GROUP = 8
F32 = jnp.float32
BF16 = jnp.bfloat16
VMEM_LIMIT = 56 * 1024 * 1024


def in_vmem():
    return pl.BlockSpec(memory_space=pltpu.VMEM)


def in_smem():
    return pl.BlockSpec(memory_space=pltpu.SMEM)


def parts(x):
    hi = x.astype(BF16)
    rest = x - hi.astype(F32)
    mid = rest.astype(BF16)
    return hi, mid, (rest - mid.astype(F32)).astype(BF16)


def mm16(a, b):
    return jnp.dot(a, b, preferred_element_type=F32)


def mm_parts(a, b):
    left = jnp.concatenate([a[0], a[0], a[1], a[0], a[1], a[2]], axis=1)
    right = jnp.concatenate([b[0], b[1], b[0], b[2], b[1], b[0]], axis=0)
    return mm16(left, right)


def mm(a, b):
    return mm_parts(parts(a), parts(b))


def pack_kernel(pred, value, variance, coord, out):
    members = pred.shape[1]
    out[:members, :] = pred[...].astype(F32).T.astype(BF16)
    rows = lax.broadcasted_iota(jnp.int32, (EXTRA, OBS_DEV), 0)
    lines = tuple(part.astype(F32) for part in parts(value[...]) + parts(variance[...]))
    place = coord[...].astype(F32)
    lines = lines + tuple(place[j : j + 1] for j in range(3))
    extra = jnp.zeros((EXTRA, OBS_DEV), F32)
    for j, line in enumerate(lines):
        extra = jnp.where(rows == j, line, extra)
    out[members:, :] = extra.astype(BF16)


def pack(pred, value, variance, coord):
    return pl.pallas_call(
        pack_kernel,
        out_shape=jax.ShapeDtypeStruct((pred.shape[1] + EXTRA, pred.shape[0]), BF16),
        in_specs=[in_vmem()] * 4,
        out_specs=in_vmem(),
        name="pack_observations",
    )(pred, value, variance, coord)


def steps_of(size):
    return size.bit_length() - 1


def relative_place(rc, rd, tiles, batches):
    nc, nd = steps_of(tiles), steps_of(batches)
    place = 0
    for s in range(nc):
        place |= ((rc >> (nc - 1 - s)) & 1) << s
    for s in range(nd):
        place |= ((rd >> (nd - 1 - s)) & 1) << (nc + s)
    return place


def swapped(block, axis, mask):
    return lax.ppermute(block, axis, [(i, i ^ mask) for i in range(lax.axis_size(axis))])


def gathered(mine, meanwhile):
    near = mine[None]
    moves = [("cell", 1 << b) for b in reversed(range(steps_of(lax.axis_size("cell"))))]
    moves += [("dp", 1 << b) for b in reversed(range(steps_of(lax.axis_size("dp"))))]
    for axis, mask in moves[:-2]:
        near = jnp.concatenate([near, swapped(near, axis, mask)], axis=0)
    near, work = meanwhile(near)
    far = swapped(near, *moves[-2])
    near_other = swapped(near, *moves[-1])
    far, work = lax.optimization_barrier((far, work))
    return (near, far, near_other, swapped(far, *moves[-1])), work


def inverse_of(eye, s, both):
    n = s.shape[0]
    bound = jnp.max(jnp.sum(jnp.abs(s), axis=0, keepdims=True))
    scale = 2.0 / (2.0 + bound)
    rho = bound / (2.0 + bound)
    r = eye - scale * (eye + s)
    both[:n] = mm(r, r)
    both[n:] = eye + r

    def more(carry):
        rho, left = carry
        return (rho > 1e-8) & (left > 0)

    def factor(carry):
        rho, left = carry
        pieces = parts(both[...])
        new = mm_parts(pieces, [p[:n] for p in pieces])
        both[:n] = new[:n]
        both[n:] += new[n:]
        return rho * rho, left - 1

    lax.while_loop(more, factor, (rho * rho, jnp.int32(40)))
    return scale * both[n:]


def chain_kernel(*refs):
    pieces, (bt_out, mp_out, oc_out, ys, wd, gs, us, both_ref) = refs[:4], refs[4:]
    batches, tiles = bt_out.shape[:2]
    members = bt_out.shape[2]
    rows = lax.broadcasted_iota(jnp.int32, (members, members), 0)
    cols = lax.broadcasted_iota(jnp.int32, (members, members), 1)
    eye = jnp.where(rows == cols, 1.0, 0.0)
    my_tile, my_batch = lax.axis_index("cell"), lax.axis_index("dp")

    for rd in range(batches):
        lefts, rights = [], []
        k = my_batch ^ rd
        for rc in range(tiles):
            r = relative_place(rc, rd, tiles, batches)
            source, r = pieces[r // pieces[0].shape[0]], r % pieces[0].shape[0]
            u = my_tile ^ rc
            raw = source[r, :members, :]
            y = raw.astype(F32)
            e = source[r, members:, :].astype(F32)
            value = e[0:1] + e[1:2] + e[2:3]
            variance = e[3:4] + e[4:5] + e[5:6]
            place = e[6:9]
            mean = jnp.mean(y, axis=0, keepdims=True)
            w = 1.0 / variance
            ew = jnp.exp(-taper_rate * jnp.sum(place * place, axis=0, keepdims=True))
            where = pl.ds(pl.multiple_of(u * OBS_DEV, OBS_DEV), OBS_DEV)
            ys[k, :, where] = raw
            wd[k, 0:1, where] = w
            wd[k, 1:2, where] = value
            wd[k, 2:3, where] = ew * (1.0 / (members - 1))
            oc_out[k, u] = jnp.concatenate([place * (2 * taper_rate * LOG2E), jnp.zeros((5, OBS_DEV), F32)], axis=0)
            z = jnp.broadcast_to((value - mean) * w, (16, OBS_DEV))
            lefts.append(jnp.concatenate(parts(jnp.concatenate([(y - mean) * w, z], axis=0)), axis=0))
            rights.append(raw)
        g = lax.dot_general(
            jnp.concatenate(lefts, axis=1), jnp.concatenate(rights, axis=1), (((1,), (1,)), ((), ())),
            preferred_element_type=F32,
        )
        n = members + 16
        g = g[:n] + g[n : 2 * n] + g[2 * n :]
        g = g - jnp.mean(g, axis=1, keepdims=True)
        gs[k] = g[:members]
        us[k] = g[members:]

    qt = eye - 1.0 / members
    p = jnp.full((16, members), 1.0 / members, F32)
    chunk = min(2, tiles) * OBS_DEV
    for k in range(batches):
        inverse = inverse_of(eye, gs[k] * (1.0 / (members - 1)), both_ref)
        inverse_parts = parts(inverse)
        qt_parts = parts(qt)
        mt = mm_parts(inverse_parts, qt_parts)
        ht = 0.5 * qt + p[0:1]
        hi, mid, lo = parts(jnp.concatenate([mt, ht], axis=0))
        twice = jnp.concatenate([hi, mid], axis=1)
        for n in range(tiles * OBS_DEV // chunk):
            where = pl.ds(n * chunk, chunk)
            y = ys[k, :, where]
            both = mm16(twice, jnp.concatenate([y, y], axis=0)) + mm16(lo, y)
            b = (both[:members] * wd[k, 2:3, where]).astype(BF16)
            pull = wd[k, 0:1, where] * (wd[k, 1:2, where] - both[members:])
            for c in range(chunk // OBS_DEV):
                u = n * (chunk // OBS_DEV) + c
                bt_out[k, u] = b[:, c * OBS_DEV : (c + 1) * OBS_DEV]
                mp_out[k, u] = pull[:, c * OBS_DEV : (c + 1) * OBS_DEV].T.astype(BF16)
        if k + 1 < batches:
            half = parts(0.5 * (eye + inverse))
            step = parts(mm_parts(parts(us[k]), inverse_parts) * (1.0 / (members - 1)))
            p = p + mm_parts(step, qt_parts)
            qt = 0.5 * (qt + mt)
            for j in range(k + 1, batches):
                g_j = parts(gs[j])
                gs[j] = mm_parts(half, parts(mm_parts(g_j, half)))
                us[j] = mm_parts(parts(us[j] - mm_parts(step, g_j)), half)


def chain(pieces, tiles, batches):
    members = pieces[0].shape[1] - EXTRA
    return pl.pallas_call(
        chain_kernel,
        out_shape=(
            jax.ShapeDtypeStruct((batches, tiles, members, OBS_DEV), BF16),
            jax.ShapeDtypeStruct((batches, tiles, OBS_DEV, members), BF16),
            jax.ShapeDtypeStruct((batches, tiles, 8, OBS_DEV), F32),
        ),
        in_specs=[in_vmem()] * 4,
        out_specs=(in_vmem(),) * 3,
        scratch_shapes=[
            pltpu.VMEM((batches, members, tiles * OBS_DEV), BF16),
            pltpu.VMEM((batches, 8, tiles * OBS_DEV), F32),
            pltpu.VMEM((batches, members, members), F32),
            pltpu.VMEM((batches, 16, members), F32),
            pltpu.VMEM((2 * members, members), F32),
        ],
        compiler_params=pltpu.CompilerParams(vmem_limit_bytes=VMEM_LIMIT),
        name="serial_transforms",
    )(*pieces)


def list_kernel(sizes_in, pairs, entries, others, *, tiles, obs_tiles):
    batches, _, slots = pairs.shape
    length = entries.shape[1]
    line = lax.broadcasted_iota(jnp.int32, (slots, slots), 1)
    down = lax.broadcasted_iota(jnp.int32, (slots, slots), 0)
    slot = lax.broadcasted_iota(jnp.int32, (slots, length), 1)

    def ones(mask, axis):
        return jnp.sum(jnp.where(mask, 1, 0), axis=axis, keepdims=True)

    row_codes = [pairs[k, 0:1, :] * obs_tiles + pairs[k, 1:2, :] for k in range(batches)]
    row_codes = jnp.concatenate(row_codes + [jnp.zeros((8 - batches, slots), jnp.int32)], axis=0)
    col_codes = row_codes.astype(F32).T.astype(jnp.int32)
    for k in range(batches):
        used = sizes_in[k]
        row = row_codes[k : k + 1]
        col = col_codes[:, k : k + 1]
        row = jnp.where(line[:1] < used, row, tiles * obs_tiles)
        col = jnp.where(down[:, :1] < used, col, tiles * obs_tiles)
        row_t, col_t = row // obs_tiles, col // obs_tiles
        same = row == col
        times = ones(same, 1)
        first_row = (ones(same & (down < line), 0) == 0) & (row_t < tiles)
        first_col = (ones(same & (line < down), 1) == 0) & (col_t < tiles)
        mates = row_t == col_t
        even_row = (ones(first_col & mates & (col < row), 0) & 1) == 0
        even_col = (ones(first_row & mates & (row < col), 1) & 1) == 0
        place = ones(first_row & even_row & (row <= col), 1) - 1
        here = first_col & (place == slot)
        value = ((col - col_t * obs_tiles) << 10) + times
        size = ones(first_row & even_row, 1)
        entry = jnp.sum(jnp.where(here & even_col, value + (col_t << 16), 0), axis=0, keepdims=True)
        other = jnp.sum(jnp.where(here & ~even_col, value, 0), axis=0, keepdims=True)
        entries[k : k + 1, :] = jnp.where(entry > 0, entry, tiles << 16)
        others[k : k + 1, :] = jnp.where(slot[:1] == length - 1, size, other)


def pair_lists(pairs, counts, tiles, obs_tiles):
    batches, slots = pairs.shape[0], pairs.shape[2]
    shape = jax.ShapeDtypeStruct((batches, -(-(slots + GROUP) // 128) * 128), jnp.int32)
    return pl.pallas_call(
        functools.partial(list_kernel, tiles=tiles, obs_tiles=obs_tiles),
        out_shape=(shape, shape),
        in_specs=[in_smem(), in_vmem()],
        out_specs=(in_vmem(),) * 2,
        cost_estimate=pl.CostEstimate(flops=40 * batches * slots * slots, bytes_accessed=16 * batches * slots, transcendentals=0),
        name="pair_lists",
    )(counts, pairs)


def cell_kernel(entries, others, state, coord, bt, mp, oc, out, acc, pert, cb, ec, held, tall):
    batches, obs_tiles = bt.shape[:2]
    members = state.shape[1]
    tiles = state.shape[0] // CT
    several = 4 if tiles % 4 == 0 else 1
    select = jnp.where(
        lax.broadcasted_iota(jnp.int32, (16, 3 * members), 1) // members
        == lax.broadcasted_iota(jnp.int32, (16, 3 * members), 0),
        1.0,
        0.0,
    ).astype(BF16)
    tall[...] = jnp.zeros(tall.shape, F32)
    tall[:3, :] = coord[...].astype(F32)

    def over_tiles(body):
        def some(i, _):
            for j in range(several):
                body(i * several + j)
            return 0

        lax.fori_loop(0, tiles // several, some, 0)

    def prepare(t):
        where = pl.ds(pl.multiple_of(t * CT, CT), CT)
        acc[t] = state[where, :].astype(F32)
        place = lax.dot_general(
            tall[:, where].astype(BF16), select, (((0,), (0,)), ((), ())), preferred_element_type=F32
        )
        norm = jnp.zeros((CT, members), F32)
        for j in range(3):
            c = place[:, j * members : (j + 1) * members]
            cb[j, t] = c
            norm = norm + c * c
        ec[t] = jnp.exp(-taper_rate * norm)

    over_tiles(prepare)
    acc[tiles] = jnp.zeros((CT, members), F32)
    pert[tiles] = jnp.zeros((CT, members), BF16)
    for j in range(3):
        cb[j, tiles] = jnp.zeros((CT, members), F32)

    for k in range(batches):

        def centre(t):
            x = acc[t]
            pert[t] = ((x - jnp.mean(x, axis=1, keepdims=True)) * ec[t]).astype(BF16)

        over_tiles(centre)

        def named(i, j):
            e, o = entries[k, i * GROUP + j], others[k, i * GROUP + j]
            return e >> 16, (e >> 10) & 63, o >> 10, e & 1023, o & 1023

        def weigh(i):
            fresh = []
            for j in range(GROUP):
                t, u0, u1, m0, m1 = named(i, j)
                score = mm16(pert[t], jnp.concatenate([bt[k, u0], bt[k, u1]], axis=1))
                halves = []
                for n, (u, m) in enumerate(((u0, m0), (u1, m1))):
                    o = oc[k, u]
                    x = cb[0, t] * o[0:1] + cb[1, t] * o[1:2] + cb[2, t] * o[2:3]
                    halves.append((jnp.exp2(x) * (score[:, n * OBS_DEV : (n + 1) * OBS_DEV] * m.astype(F32))).astype(BF16))
                fresh.append(halves)
            for j in range(GROUP):
                held[j, :, :OBS_DEV] = fresh[j][0]
                held[j, :, OBS_DEV:] = fresh[j][1]

        def pull(i):
            for j in range(GROUP):
                t, u0, u1, _, _ = named(i, j)
                acc[t] += mm16(held[j], jnp.concatenate([mp[k, u0], mp[k, u1]], axis=0))

        def group(i, _):
            pull(i - 1)
            weigh(i)
            return 0

        groups = (others[k, others.shape[1] - 1] + GROUP - 1) // GROUP
        weigh(0)
        lax.fori_loop(1, groups, group, 0)
        pull(groups - 1)

    def finish(t):
        out[pl.ds(pl.multiple_of(t * CT, CT), CT), :] = acc[t].astype(BF16)

    over_tiles(finish)


def cells(entries, others, state, coord, bt, mp, oc):
    members = state.shape[1]
    tiles = state.shape[0] // CT
    return pl.pallas_call(
        cell_kernel,
        out_shape=jax.ShapeDtypeStruct(state.shape, BF16),
        in_specs=[in_smem()] * 2 + [in_vmem()] * 5,
        out_specs=in_vmem(),
        scratch_shapes=[
            pltpu.VMEM((tiles + 1, CT, members), F32),
            pltpu.VMEM((tiles + 1, CT, members), BF16),
            pltpu.VMEM((3, tiles + 1, CT, members), F32),
            pltpu.VMEM((tiles, CT, members), F32),
            pltpu.VMEM((GROUP, CT, 2 * OBS_DEV), BF16),
            pltpu.VMEM((16, tiles * CT), F32),
        ],
        compiler_params=pltpu.CompilerParams(vmem_limit_bytes=VMEM_LIMIT),
        name="cell_updates",
    )(entries, others, state, coord, bt, mp, oc)


def local(
    state,
    cell_coordinate,
    member_predictions,
    measured_values,
    obs_error_variance,
    observation_coordinate,
    localization_tile_pairs,
    used_pair_count,
):
    obs_tiles = lax.axis_size("cell")
    batches = lax.axis_size("dp")
    tiles = state.shape[0] // CT
    mine = pack(member_predictions[0], measured_values, obs_error_variance, observation_coordinate[0])

    def meanwhile(near):
        near, pairs, counts = lax.optimization_barrier((near, localization_tile_pairs[0], used_pair_count[0]))
        return near, pair_lists(pairs, counts, tiles, obs_tiles)

    pieces, (entries, others) = gathered(mine, meanwhile)
    bt, mp, oc = chain(pieces, obs_tiles, batches)
    return cells(entries, others, state, cell_coordinate, bt, mp, oc)


def solution(mesh):
    placed = (
        P(("cell", "dp"), None),
        P(None, ("cell", "dp")),
        P("dp", "cell", None),
        P("dp", "cell"),
        P("dp", "cell"),
        P("dp", None, "cell"),
        P(("cell", "dp"), None, None, None),
        P(("cell", "dp"), None),
    )
    return jax.shard_map(
        local, mesh=mesh, in_specs=placed, out_specs=P(("cell", "dp"), None), check_vma=False
    )
```

profile of v0, /device:TPU:3, one launch (start us, length us, event | category | flops | bytes accessed | tf_op | source)
XLA Modules:
  0.0 81.4 jit_solution(8635330917484060656)
XLA Ops:
  0.0 1.5 %pack_observations.1 = bf16[144,128]{1,0:T(8,128)(2,1)} custom-call(bf16[128,128]{1,0:T(8,128)(2,1)} %bitcast.9, f32[1,128]{1,0:T(1,128)} %value.1, f32[1,128]{1,0:T(1,128)} %variance.1, bf16[3,128]{1,0:T(4,128)(2,1)} %bitcast.10), custom_call_target="tpu_custom_call" | custom-call | tf_op jit(solution)/shard_map/pack_observations/pallas_call | solution.py:65
  1.5 2.3 %collective-permute-start = (bf16[1,144,128]{2,1,0:T(8,128)(2,1)}, bf16[1,144,128]{2,1,0:T(8,128)(2,1)S(1)}, u32[]{:S(2)}, u32[]{:S(2)}) collective-permute-start(bf16[1,144,128]{2,1,0:T(8,128)(2,1)} %bitcast.5), channel_id=1, source_target_pairs={{0,16},{4,20},{8,24},{12,28},{16,0},{20,4},{24,8},{28,12},{1,17},{... | collective-permute-start | bytes 110600 | tf_op jit(solution)/shard_map/ppermute | solution.py:89
  3.8 1.6 %collective-permute-done = bf16[1,144,128]{2,1,0:T(8,128)(2,1)S(1)} collective-permute-done((bf16[1,144,128]{2,1,0:T(8,128)(2,1)}, bf16[1,144,128]{2,1,0:T(8,128)(2,1)S(1)}, u32[]{:S(2)}, u32[]{:S(2)}) %collective-permute-start) | collective-permute-done | bytes 36896 | tf_op jit(solution)/shard_map/ppermute | solution.py:89
  5.4 0.8 pad_maximum_fusion.2
  6.2 1.3 %collective-permute-start.1 = (bf16[2,144,128]{2,1,0:T(8,128)(2,1)S(1)}, bf16[2,144,128]{2,1,0:T(8,128)(2,1)S(1)}, u32[]{:S(2)}, u32[]{:S(2)}) collective-permute-start(bf16[2,144,128]{2,1,0:T(8,128)(2,1)S(1)} %pad_maximum_fusion.2), channel_id=1, source_target_pairs={{0,8},{4,12},{8,0},{12,4},{16,24},{20,28},{24,16},{28,20},{1,9},{5... | collective-permute-start | bytes 221192 | tf_op jit(solution)/shard_map/ppermute | solution.py:89
  7.5 1.9 %collective-permute-done.1 = bf16[2,144,128]{2,1,0:T(8,128)(2,1)S(1)} collective-permute-done((bf16[2,144,128]{2,1,0:T(8,128)(2,1)S(1)}, bf16[2,144,128]{2,1,0:T(8,128)(2,1)S(1)}, u32[]{:S(2)}, u32[]{:S(2)}) %collective-permute-start.1) | collective-permute-done | bytes 73760 | tf_op jit(solution)/shard_map/ppermute | solution.py:89
  9.4 0.8 pad_maximum_fusion.1
  10.2 1.3 %collective-permute-start.2 = (bf16[4,144,128]{2,1,0:T(8,128)(2,1)S(1)}, bf16[4,144,128]{2,1,0:T(8,128)(2,1)S(1)}, u32[]{:S(2)}, u32[]{:S(2)}) collective-permute-start(bf16[4,144,128]{2,1,0:T(8,128)(2,1)S(1)} %pad_maximum_fusion.1), channel_id=1, source_target_pairs={{0,4},{4,0},{8,12},{12,8},{16,20},{20,16},{24,28},{28,24},{1,5},{5... | collective-permute-start | bytes 442376 | tf_op jit(solution)/shard_map/ppermute | solution.py:89
  11.5 2.8 %collective-permute-done.2 = bf16[4,144,128]{2,1,0:T(8,128)(2,1)S(1)} collective-permute-done((bf16[4,144,128]{2,1,0:T(8,128)(2,1)S(1)}, bf16[4,144,128]{2,1,0:T(8,128)(2,1)S(1)}, u32[]{:S(2)}, u32[]{:S(2)}) %collective-permute-start.2) | collective-permute-done | bytes 147488 | tf_op jit(solution)/shard_map/ppermute | solution.py:89
  14.2 0.8 pad_maximum_fusion.refs_0_
  15.0 0.0 copy-start
  15.1 0.3 collective-permute-start.3
  15.3 4.5 %collective-permute-start.4 = (bf16[8,144,128]{2,1,0:T(8,128)(2,1)S(1)}, bf16[8,144,128]{2,1,0:T(8,128)(2,1)S(1)}, u32[]{:S(2)}, u32[]{:S(2)}) collective-permute-start(bf16[8,144,128]{2,1,0:T(8,128)(2,1)S(1)} %pad_maximum_fusion.refs_0_), channel_id=1, source_target_pairs={{0,1},{1,0},{2,3},{3,2},{4,5},{5,4},{6,7},{7,6},{8,9},{9,8},{10,11... | collective-permute-start | bytes 884744 | tf_op jit(solution)/shard_map/ppermute | solution.py:89
  19.8 4.2 %pair_lists.1 = (s32[4,384]{1,0:T(4,128)}, s32[4,384]{1,0:T(4,128)}) custom-call(s32[4]{0:T(128)} %bitcast.12, s32[4,2,256]{2,1,0:T(2,128)} %bitcast.11), custom_call_target="tpu_custom_call" | custom-call | flops 10485760 | bytes 16384 | tf_op jit(solution)/shard_map/pair_lists/pallas_call | solution.py:269
  24.1 0.0 collective-permute-done.3.refs_1_
  24.1 2.2 %collective-permute-start.5 = (bf16[8,144,128]{2,1,0:T(8,128)(2,1)S(1)}, bf16[8,144,128]{2,1,0:T(8,128)(2,1)S(1)}, u32[]{:S(2)}, u32[]{:S(2)}) collective-permute-start(bf16[8,144,128]{2,1,0:T(8,128)(2,1)S(1)} %collective-permute-done.3.refs_1_), channel_id=1, source_target_pairs={{0,1},{1,0},{2,3},{3,2},{4,5},{5,4},{6,7},{7,6},{8,9},{9,8},{10,11... | collective-permute-start | bytes 884744 | tf_op jit(solution)/shard_map/ppermute | solution.py:89
  26.2 0.0 collective-permute-done.4.refs_2_
  26.2 1.2 %collective-permute-done.5.refs_3_ = bf16[8,144,128]{2,1,0:T(8,128)(2,1)S(1)} collective-permute-done((bf16[8,144,128]{2,1,0:T(8,128)(2,1)S(1)}, bf16[8,144,128]{2,1,0:T(8,128)(2,1)S(1)}, u32[]{:S(2)}, u32[]{:S(2)}) %collective-permute-start.5) | collective-permute-done | bytes 294944 | tf_op jit(solution)/shard_map/ppermute | solution.py:89
  27.5 0.0 copy-done
  27.5 0.0 copy-done.1
  27.5 0.0 copy-done.2
  27.5 0.7 copy-done.3
  28.2 15.9 %serial_transforms.1 = (bf16[4,8,128,128]{3,2,1,0:T(8,128)(2,1)}, bf16[4,8,128,128]{3,2,1,0:T(8,128)(2,1)}, f32[4,8,8,128]{3,2,1,0:T(8,128)}) custom-call(bf16[8,144,128]{2,1,0:T(8,128)(2,1)} %copy-done, bf16[8,144,128]{2,1,0:T(8,128)(2,1)} %copy-done.1, bf16[8,144,128]{2,1,0:T(8,128)(2,1)} %copy-done.2, bf16[8,144,128]{2,1,0:T(8,128)(2,1)} %copy-done.3), custom_call_target="tpu_custom_call" | custom-call | tf_op jit(solution)/shard_map/serial_transforms/pallas_call | solution.py:208
  44.1 37.3 %cell_updates.1 = bf16[5120,128]{1,0:T(8,128)(2,1)} custom-call(s32[4,384]{1,0:T(4,128)} %get-tuple-element.21.entries, s32[4,384]{1,0:T(4,128)} %get-tuple-element.22.others, bf16[5120,128]{1,0:T(8,128)(2,1)} %state.1, bf16[3,5120]{1,0:T(4,128)(2,1)} %coord.1, bf16[4,8,128,128]{3,2,1,0:T(8,128)(2,1)} %get-tuple-element.24.bt, ...), custom_call_target="tpu_custom_call" | custom-call | tf_op jit(solution)/shard_map/cell_updates/pallas_call | solution.py:371
  (3 shorter events, 0.0 us)
Async XLA Ops:
  1.5 3.9 %collective-permute-start = (bf16[1,144,128]{2,1,0:T(8,128)(2,1)}, bf16[1,144,128]{2,1,0:T(8,128)(2,1)S(1)}, u32[]{:S(2)}, u32[]{:S(2)}) collective-permute-start(bf16[1,144,128]{2,1,0:T(8,128)(2,1)} %bitcast.5), channel_id=1, source_target_pairs={{0,16},{4,20},{8,24},{12,28},{16,0},{20,4},{24,8},{28,12},{1,17},{... | collective-permute-start | bytes 110600 | tf_op jit(solution)/shard_map/ppermute | solution.py:89
  6.2 3.2 %collective-permute-start.1 = (bf16[2,144,128]{2,1,0:T(8,128)(2,1)S(1)}, bf16[2,144,128]{2,1,0:T(8,128)(2,1)S(1)}, u32[]{:S(2)}, u32[]{:S(2)}) collective-permute-start(bf16[2,144,128]{2,1,0:T(8,128)(2,1)S(1)} %pad_maximum_fusion.2), channel_id=1, source_target_pairs={{0,8},{4,12},{8,0},{12,4},{16,24},{20,28},{24,16},{28,20},{1,9},{5... | collective-permute-start | bytes 221192 | tf_op jit(solution)/shard_map/ppermute | solution.py:89
  10.2 4.1 %collective-permute-start.2 = (bf16[4,144,128]{2,1,0:T(8,128)(2,1)S(1)}, bf16[4,144,128]{2,1,0:T(8,128)(2,1)S(1)}, u32[]{:S(2)}, u32[]{:S(2)}) collective-permute-start(bf16[4,144,128]{2,1,0:T(8,128)(2,1)S(1)} %pad_maximum_fusion.1), channel_id=1, source_target_pairs={{0,4},{4,0},{8,12},{12,8},{16,20},{20,16},{24,28},{28,24},{1,5},{5... | collective-permute-start | bytes 442376 | tf_op jit(solution)/shard_map/ppermute | solution.py:89
  15.0 12.4 %copy-start = (bf16[8,144,128]{2,1,0:T(8,128)(2,1)}, bf16[8,144,128]{2,1,0:T(8,128)(2,1)S(1)}, u32[]{:S(2)}) copy-start(bf16[8,144,128]{2,1,0:T(8,128)(2,1)S(1)} %pad_maximum_fusion.refs_0_) | copy-start | bytes 884740
  15.1 9.0 %collective-permute-start.3 = (bf16[8,144,128]{2,1,0:T(8,128)(2,1)S(1)}, bf16[8,144,128]{2,1,0:T(8,128)(2,1)S(1)}, u32[]{:S(2)}, u32[]{:S(2)}) collective-permute-start(bf16[8,144,128]{2,1,0:T(8,128)(2,1)S(1)} %pad_maximum_fusion.refs_0_), channel_id=1, source_target_pairs={{0,2},{1,3},{2,0},{3,1},{4,6},{5,7},{6,4},{7,5},{8,10},{9,11},{10,... | collective-permute-start | bytes 884744 | tf_op jit(solution)/shard_map/ppermute | solution.py:89
  15.3 10.9 %collective-permute-start.4 = (bf16[8,144,128]{2,1,0:T(8,128)(2,1)S(1)}, bf16[8,144,128]{2,1,0:T(8,128)(2,1)S(1)}, u32[]{:S(2)}, u32[]{:S(2)}) collective-permute-start(bf16[8,144,128]{2,1,0:T(8,128)(2,1)S(1)} %pad_maximum_fusion.refs_0_), channel_id=1, source_target_pairs={{0,1},{1,0},{2,3},{3,2},{4,5},{5,4},{6,7},{7,6},{8,9},{9,8},{10,11... | collective-permute-start | bytes 884744 | tf_op jit(solution)/shard_map/ppermute | solution.py:89
  24.1 3.4 %copy-start.1 = (bf16[8,144,128]{2,1,0:T(8,128)(2,1)}, bf16[8,144,128]{2,1,0:T(8,128)(2,1)S(1)}, u32[]{:S(2)}) copy-start(bf16[8,144,128]{2,1,0:T(8,128)(2,1)S(1)} %collective-permute-done.3.refs_1_) | copy-start | bytes 884740
  24.1 3.4 %collective-permute-start.5 = (bf16[8,144,128]{2,1,0:T(8,128)(2,1)S(1)}, bf16[8,144,128]{2,1,0:T(8,128)(2,1)S(1)}, u32[]{:S(2)}, u32[]{:S(2)}) collective-permute-start(bf16[8,144,128]{2,1,0:T(8,128)(2,1)S(1)} %collective-permute-done.3.refs_1_), channel_id=1, source_target_pairs={{0,1},{1,0},{2,3},{3,2},{4,5},{5,4},{6,7},{7,6},{8,9},{9,8},{10,11... | collective-permute-start | bytes 884744 | tf_op jit(solution)/shard_map/ppermute | solution.py:89
  26.2 1.2 %copy-start.2 = (bf16[8,144,128]{2,1,0:T(8,128)(2,1)}, bf16[8,144,128]{2,1,0:T(8,128)(2,1)S(1)}, u32[]{:S(2)}) copy-start(bf16[8,144,128]{2,1,0:T(8,128)(2,1)S(1)} %collective-permute-done.4.refs_2_) | copy-start | bytes 884740
  27.5 0.7 copy-start.3
where the time goes:
time: 82.2 us; the launch traced here: 81.4 us
  Pallas kernels  59 us (72%)
  starting transfers between devices  11.9 us (14%)
  waiting for transfers between devices  7.45 us (9%)
  other arithmetic  2.36 us (3%)
    pallas_call x1, Pallas kernels, cells(): pl.pallas_call(cell_kernel, out_shape=jax.ShapeDtypeStruct(state.shape, B...  37.3 us
    pallas_call x1, Pallas kernels, chain(): pl.pallas_call(chain_kernel, out_shape=(jax.ShapeDtypeStruct((batches, ti...  15.9 us
    ppermute x6, starting transfers between devices, swapped(): lax.ppermute(block, axis, [(i, i ^ mask) for i in range(lax.axis_size(axi...  11.9 us
    ppermute x6, waiting for transfers between devices, swapped(): lax.ppermute(block, axis, [(i, i ^ mask) for i in range(lax.axis_size(axi...  7.45 us
    pallas_call x1, Pallas kernels, pair_lists(): pl.pallas_call(functools.partial(list_kernel, tiles=tiles, obs_tiles=obs_...  4.22 us
    concatenate x3, other arithmetic, gathered(): near = jnp.concatenate([near, swapped(near, axis, mask)], axis=0)  2.36 us
  transfers between devices with their start and end apart: 6, of which 4 were waited for; matrix products, arithmetic and copies ran while one was open for 0% of the time, Pallas kernels for 5%

commit v1 on v0

--- a/solution.py
+++ b/solution.py
@@ -51,14 +51,9 @@
 def pack_kernel(pred, value, variance, coord, out):
     members = pred.shape[1]
     out[:members, :] = pred[...].astype(F32).T.astype(BF16)
-    rows = lax.broadcasted_iota(jnp.int32, (EXTRA, OBS_DEV), 0)
-    lines = tuple(part.astype(F32) for part in parts(value[...]) + parts(variance[...]))
     place = coord[...].astype(F32)
-    lines = lines + tuple(place[j : j + 1] for j in range(3))
-    extra = jnp.zeros((EXTRA, OBS_DEV), F32)
-    for j, line in enumerate(lines):
-        extra = jnp.where(rows == j, line, extra)
-    out[members:, :] = extra.astype(BF16)
+    lines = parts(value[...]) + parts(variance[...]) + tuple(place[j : j + 1] for j in range(3))
+    out[members:, :] = stacked(lines).astype(BF16)
 
 
 def pack(pred, value, variance, coord):
@@ -71,35 +66,23 @@
     )(pred, value, variance, coord)
 
 
-def steps_of(size):
-    return size.bit_length() - 1
-
-
-def relative_place(rc, rd, tiles, batches):
-    nc, nd = steps_of(tiles), steps_of(batches)
-    place = 0
-    for s in range(nc):
-        place |= ((rc >> (nc - 1 - s)) & 1) << s
-    for s in range(nd):
-        place |= ((rd >> (nd - 1 - s)) & 1) << (nc + s)
-    return place
-
-
 def swapped(block, axis, mask):
     return lax.ppermute(block, axis, [(i, i ^ mask) for i in range(lax.axis_size(axis))])
 
 
 def gathered(mine, meanwhile):
-    near = mine[None]
-    moves = [("cell", 1 << b) for b in reversed(range(steps_of(lax.axis_size("cell"))))]
-    moves += [("dp", 1 << b) for b in reversed(range(steps_of(lax.axis_size("dp"))))]
-    for axis, mask in moves[:-2]:
-        near = jnp.concatenate([near, swapped(near, axis, mask)], axis=0)
-    near, work = meanwhile(near)
-    far = swapped(near, *moves[-2])
-    near_other = swapped(near, *moves[-1])
-    far, work = lax.optimization_barrier((far, work))
-    return (near, far, near_other, swapped(far, *moves[-1])), work
+    near = [mine[None]]
+    near += [swapped(near[0], "cell", mask) for mask in range(1, lax.axis_size("cell"))]
+    near, work = meanwhile(jnp.concatenate(near, axis=0))
+    pieces = {0: near}
+    mask = lax.axis_size("dp") // 2
+    while mask:
+        for d in list(pieces):
+            pieces[d ^ mask] = swapped(pieces[d], "dp", mask)
+        if len(pieces) == 2:
+            pieces[mask], work = lax.optimization_barrier((pieces[mask], work))
+        mask //= 2
+    return [pieces[d] for d in range(len(pieces))], work
 
 
 def inverse_of(eye, s, both):
@@ -107,9 +90,16 @@
     bound = jnp.max(jnp.sum(jnp.abs(s), axis=0, keepdims=True))
     scale = 2.0 / (2.0 + bound)
     rho = bound / (2.0 + bound)
-    r = eye - scale * (eye + s)
-    both[:n] = mm(r, r)
-    both[n:] = eye + r
+    both[:n] = eye - scale * (eye + s)
+
+    def advance(rho, square, total):
+        by = 1.0 / (2.0 - rho * rho)
+        both[:n] = (2.0 * by) * square - (rho * rho * by) * eye
+        both[n:] = (2.0 * by) * total
+        return rho * rho * by
+
+    r = both[:n]
+    rho = advance(rho, mm(r, r), eye + r)
 
     def more(carry):
         rho, left = carry
@@ -117,18 +107,42 @@
 
     def factor(carry):
         rho, left = carry
-        pieces = parts(both[...])
+        old = both[...]
+        pieces = parts(old)
         new = mm_parts(pieces, [p[:n] for p in pieces])
-        both[:n] = new[:n]
-        both[n:] += new[n:]
-        return rho * rho, left - 1
-
-    lax.while_loop(more, factor, (rho * rho, jnp.int32(40)))
+        return advance(rho, new[:n], old[n:] + new[n:]), left - 1
+
+    lax.while_loop(more, factor, (rho, jnp.int32(40)))
     return scale * both[n:]
 
 
+def stacked(lines):
+    width = lines[0].shape[1]
+    rows = lax.broadcasted_iota(jnp.int32, (16, width), 0)
+    out = jnp.zeros((16, width), F32)
+    for j, line in enumerate(lines):
+        out = jnp.where(rows == j, line.astype(F32), out)
+    return out
+
+
+def norm_parts(place):
+    return parts(-taper_rate * LOG2E * jnp.sum(place * place, axis=0, keepdims=True))
+
+
+def cell_features(place):
+    ones = [jnp.ones((1, place.shape[1]), F32)] * 3
+    return stacked([place[j : j + 1] for j in range(3)] * 3 + list(norm_parts(place)) + ones)
+
+
+def obs_features(place):
+    ones = [jnp.ones((1, place.shape[1]), F32)] * 3
+    scaled = parts(place * (2 * taper_rate * LOG2E))
+    lines = [part[j : j + 1].astype(F32) for part in scaled for j in range(3)]
+    return stacked(lines + ones + list(norm_parts(place))).astype(BF16)
+
+
 def chain_kernel(*refs):
-    pieces, (bt_out, mp_out, oc_out, ys, wd, gs, us, both_ref) = refs[:4], refs[4:]
+    pieces, (bt_out, mp_out, of_out, ys, wd, gs, us, both_ref) = refs[:-8], refs[-8:]
     batches, tiles = bt_out.shape[:2]
     members = bt_out.shape[2]
     rows = lax.broadcasted_iota(jnp.int32, (members, members), 0)
@@ -140,24 +154,20 @@
         lefts, rights = [], []
         k = my_batch ^ rd
         for rc in range(tiles):
-            r = relative_place(rc, rd, tiles, batches)
-            source, r = pieces[r // pieces[0].shape[0]], r % pieces[0].shape[0]
             u = my_tile ^ rc
-            raw = source[r, :members, :]
+            raw = pieces[rd][rc, :members, :]
             y = raw.astype(F32)
-            e = source[r, members:, :].astype(F32)
+            e = pieces[rd][rc, members:, :].astype(F32)
             value = e[0:1] + e[1:2] + e[2:3]
             variance = e[3:4] + e[4:5] + e[5:6]
             place = e[6:9]
             mean = jnp.mean(y, axis=0, keepdims=True)
             w = 1.0 / variance
-            ew = jnp.exp(-taper_rate * jnp.sum(place * place, axis=0, keepdims=True))
             where = pl.ds(pl.multiple_of(u * OBS_DEV, OBS_DEV), OBS_DEV)
             ys[k, :, where] = raw
             wd[k, 0:1, where] = w
             wd[k, 1:2, where] = value
-            wd[k, 2:3, where] = ew * (1.0 / (members - 1))
-            oc_out[k, u] = jnp.concatenate([place * (2 * taper_rate * LOG2E), jnp.zeros((5, OBS_DEV), F32)], axis=0)
+            of_out[k, u] = obs_features(place)
             z = jnp.broadcast_to((value - mean) * w, (16, OBS_DEV))
             lefts.append(jnp.concatenate(parts(jnp.concatenate([(y - mean) * w, z], axis=0)), axis=0))
             rights.append(raw)
@@ -186,7 +196,7 @@
             where = pl.ds(n * chunk, chunk)
             y = ys[k, :, where]
             both = mm16(twice, jnp.concatenate([y, y], axis=0)) + mm16(lo, y)
-            b = (both[:members] * wd[k, 2:3, where]).astype(BF16)
+            b = (both[:members] * (1.0 / (members - 1))).astype(BF16)
             pull = wd[k, 0:1, where] * (wd[k, 1:2, where] - both[members:])
             for c in range(chunk // OBS_DEV):
                 u = n * (chunk // OBS_DEV) + c
@@ -210,9 +220,9 @@
         out_shape=(
             jax.ShapeDtypeStruct((batches, tiles, members, OBS_DEV), BF16),
             jax.ShapeDtypeStruct((batches, tiles, OBS_DEV, members), BF16),
-            jax.ShapeDtypeStruct((batches, tiles, 8, OBS_DEV), F32),
+            jax.ShapeDtypeStruct((batches, tiles, 16, OBS_DEV), BF16),
         ),
-        in_specs=[in_vmem()] * 4,
+        in_specs=[in_vmem()] * len(pieces),
         out_specs=(in_vmem(),) * 3,
         scratch_shapes=[
             pltpu.VMEM((batches, members, tiles * OBS_DEV), BF16),
@@ -276,19 +286,12 @@
     )(counts, pairs)
 
 
-def cell_kernel(entries, others, state, coord, bt, mp, oc, out, acc, pert, cb, ec, held, tall):
+def cell_kernel(entries, others, state, coord, bt, mp, of, out, acc, pert, feat, held, tall):
     batches, obs_tiles = bt.shape[:2]
     members = state.shape[1]
     tiles = state.shape[0] // CT
     several = 4 if tiles % 4 == 0 else 1
-    select = jnp.where(
-        lax.broadcasted_iota(jnp.int32, (16, 3 * members), 1) // members
-        == lax.broadcasted_iota(jnp.int32, (16, 3 * members), 0),
-        1.0,
-        0.0,
-    ).astype(BF16)
-    tall[...] = jnp.zeros(tall.shape, F32)
-    tall[:3, :] = coord[...].astype(F32)
+    tall[...] = cell_features(coord[...].astype(F32))
 
     def over_tiles(body):
         def some(i, _):
@@ -301,27 +304,18 @@
     def prepare(t):
         where = pl.ds(pl.multiple_of(t * CT, CT), CT)
         acc[t] = state[where, :].astype(F32)
-        place = lax.dot_general(
-            tall[:, where].astype(BF16), select, (((0,), (0,)), ((), ())), preferred_element_type=F32
-        )
-        norm = jnp.zeros((CT, members), F32)
-        for j in range(3):
-            c = place[:, j * members : (j + 1) * members]
-            cb[j, t] = c
-            norm = norm + c * c
-        ec[t] = jnp.exp(-taper_rate * norm)
+        feat[t] = tall[:, where].T.astype(BF16)
 
     over_tiles(prepare)
     acc[tiles] = jnp.zeros((CT, members), F32)
     pert[tiles] = jnp.zeros((CT, members), BF16)
-    for j in range(3):
-        cb[j, tiles] = jnp.zeros((CT, members), F32)
+    feat[tiles] = jnp.zeros((CT, 16), BF16)
 
     for k in range(batches):
 
         def centre(t):
             x = acc[t]
-            pert[t] = ((x - jnp.mean(x, axis=1, keepdims=True)) * ec[t]).astype(BF16)
+            pert[t] = ((x - jnp.mean(x, axis=1, keepdims=True))).astype(BF16)
 
         over_tiles(centre)
 
@@ -330,19 +324,14 @@
             return e >> 16, (e >> 10) & 63, o >> 10, e & 1023, o & 1023
 
         def weigh(i):
-            fresh = []
             for j in range(GROUP):
                 t, u0, u1, m0, m1 = named(i, j)
                 score = mm16(pert[t], jnp.concatenate([bt[k, u0], bt[k, u1]], axis=1))
-                halves = []
-                for n, (u, m) in enumerate(((u0, m0), (u1, m1))):
-                    o = oc[k, u]
-                    x = cb[0, t] * o[0:1] + cb[1, t] * o[1:2] + cb[2, t] * o[2:3]
-                    halves.append((jnp.exp2(x) * (score[:, n * OBS_DEV : (n + 1) * OBS_DEV] * m.astype(F32))).astype(BF16))
-                fresh.append(halves)
-            for j in range(GROUP):
-                held[j, :, :OBS_DEV] = fresh[j][0]
-                held[j, :, OBS_DEV:] = fresh[j][1]
+                power = mm16(feat[t], jnp.concatenate([of[k, u0], of[k, u1]], axis=1))
+                taper = jnp.exp2(power)
+                for n, m in enumerate((m0, m1)):
+                    cut = slice(n * OBS_DEV, (n + 1) * OBS_DEV)
+                    held[j, :, cut] = (taper[:, cut] * (score[:, cut] * m.astype(F32))).astype(BF16)
 
         def pull(i):
             for j in range(GROUP):
@@ -365,7 +354,7 @@
     over_tiles(finish)
 
 
-def cells(entries, others, state, coord, bt, mp, oc):
+def cells(entries, others, state, coord, bt, mp, of):
     members = state.shape[1]
     tiles = state.shape[0] // CT
     return pl.pallas_call(
@@ -376,14 +365,13 @@
         scratch_shapes=[
             pltpu.VMEM((tiles + 1, CT, members), F32),
             pltpu.VMEM((tiles + 1, CT, members), BF16),
-            pltpu.VMEM((3, tiles + 1, CT, members), F32),
-            pltpu.VMEM((tiles, CT, members), F32),
+            pltpu.VMEM((tiles + 1, CT, 16), BF16),
             pltpu.VMEM((GROUP, CT, 2 * OBS_DEV), BF16),
             pltpu.VMEM((16, tiles * CT), F32),
         ],
         compiler_params=pltpu.CompilerParams(vmem_limit_bytes=VMEM_LIMIT),
         name="cell_updates",
-    )(entries, others, state, coord, bt, mp, oc)
+    )(entries, others, state, coord, bt, mp, of)
 
 
 def local(
@@ -406,8 +394,8 @@
         return near, pair_lists(pairs, counts, tiles, obs_tiles)
 
     pieces, (entries, others) = gathered(mine, meanwhile)
-    bt, mp, oc = chain(pieces, obs_tiles, batches)
-    return cells(entries, others, state, cell_coordinate, bt, mp, oc)
+    bt, mp, of = chain(pieces, obs_tiles, batches)
+    return cells(entries, others, state, cell_coordinate, bt, mp, of)
 
 
 def solution(mesh):

time: 82.2 us -> 80.9 us (0.984)
  the two profiles are of different devices: /device:TPU:3 before, /device:TPU:25 now
where the time goes in v1:
time: 80.9 us; the launch traced here: 81.7 us
  Pallas kernels  55.3 us (68%)
  starting transfers between devices  16 us (20%)
  waiting for transfers between devices  8.68 us (11%)
  local copies, waits for them, and re-layouts  1.61 us (2%)
    pallas_call x1, Pallas kernels, cells(): pl.pallas_call(cell_kernel, out_shape=jax.ShapeDtypeStruct(state.shape, B...  35 us
    ppermute x10, starting transfers between devices, swapped(): lax.ppermute(block, axis, [(i, i ^ mask) for i in range(lax.axis_size(axi...  16 us
    pallas_call x1, Pallas kernels, chain(): pl.pallas_call(chain_kernel, out_shape=(jax.ShapeDtypeStruct((batches, ti...  14.6 us
    ppermute x10, waiting for transfers between devices, swapped(): lax.ppermute(block, axis, [(i, i ^ mask) for i in range(lax.axis_size(axi...  8.68 us
    pallas_call x1, Pallas kernels, pair_lists(): pl.pallas_call(functools.partial(list_kernel, tiles=tiles, obs_tiles=obs_...  4.22 us
  transfers between devices with their start and end apart: 10, of which 4 were waited for; matrix products, arithmetic and copies ran while one was open for 1% of the time, Pallas kernels for 5%

profile of v1, /device:TPU:25, one launch (start us, length us, event | category | flops | bytes accessed | tf_op | source)
XLA Modules:
  0.0 81.7 jit_solution(3555660945119934579)
XLA Ops:
  0.0 1.5 %pack_observations.1 = bf16[144,128]{1,0:T(8,128)(2,1)} custom-call(bf16[128,128]{1,0:T(8,128)(2,1)} %bitcast.13, f32[1,128]{1,0:T(1,128)} %value.1, f32[1,128]{1,0:T(1,128)} %variance.1, bf16[3,128]{1,0:T(4,128)(2,1)} %bitcast.14), custom_call_target="tpu_custom_call" | custom-call | tf_op jit(solution)/shard_map/pack_observations/pallas_call | solution.py:60
  1.5 0.9 %collective-permute-start.6 = (bf16[1,144,128]{2,1,0:T(8,128)(2,1)}, bf16[1,144,128]{2,1,0:T(8,128)(2,1)S(1)}, u32[]{:S(2)}, u32[]{:S(2)}) collective-permute-start(bf16[1,144,128]{2,1,0:T(8,128)(2,1)} %bitcast.6), channel_id=1, source_target_pairs={{0,28},{4,24},{8,20},{12,16},{16,12},{20,8},{24,4},{28,0},{1,29},{... | collective-permute-start | bytes 110600 | tf_op jit(solution)/shard_map/ppermute | solution.py:70
  2.4 3.3 %collective-permute-start.5 = (bf16[1,144,128]{2,1,0:T(8,128)(2,1)}, bf16[1,144,128]{2,1,0:T(8,128)(2,1)S(1)}, u32[]{:S(2)}, u32[]{:S(2)}) collective-permute-start(bf16[1,144,128]{2,1,0:T(8,128)(2,1)} %bitcast.7), channel_id=1, source_target_pairs={{0,24},{4,28},{8,16},{12,20},{16,8},{20,12},{24,0},{28,4},{1,25},{... | collective-permute-start | bytes 110600 | tf_op jit(solution)/shard_map/ppermute | solution.py:70
  5.7 0.0 collective-permute-start.4
  5.7 2.3 %collective-permute-start.3 = (bf16[1,144,128]{2,1,0:T(8,128)(2,1)}, bf16[1,144,128]{2,1,0:T(8,128)(2,1)S(1)}, u32[]{:S(2)}, u32[]{:S(2)}) collective-permute-start(bf16[1,144,128]{2,1,0:T(8,128)(2,1)} %bitcast.9), channel_id=1, source_target_pairs={{0,16},{4,20},{8,24},{12,28},{16,0},{20,4},{24,8},{28,12},{1,17},{... | collective-permute-start | bytes 110600 | tf_op jit(solution)/shard_map/ppermute | solution.py:70
  8.0 1.2 %collective-permute-start = (bf16[1,144,128]{2,1,0:T(8,128)(2,1)}, bf16[1,144,128]{2,1,0:T(8,128)(2,1)S(1)}, u32[]{:S(2)}, u32[]{:S(2)}) collective-permute-start(bf16[1,144,128]{2,1,0:T(8,128)(2,1)} %bitcast.10), channel_id=1, source_target_pairs={{0,4},{4,0},{8,12},{12,8},{16,20},{20,16},{24,28},{28,24},{1,5},{5... | collective-permute-start | bytes 110600 | tf_op jit(solution)/shard_map/ppermute | solution.py:70
  9.3 0.8 constant_dynamic-update-slice_fusion.7
  10.1 1.3 %collective-permute-done = bf16[1,144,128]{2,1,0:T(8,128)(2,1)S(1)} collective-permute-done((bf16[1,144,128]{2,1,0:T(8,128)(2,1)}, bf16[1,144,128]{2,1,0:T(8,128)(2,1)S(1)}, u32[]{:S(2)}, u32[]{:S(2)}) %collective-permute-start) | collective-permute-done | bytes 36896 | tf_op jit(solution)/shard_map/ppermute | solution.py:70
  11.4 0.0 collective-permute-start.1
  11.4 3.0 %collective-permute-done.1 = bf16[1,144,128]{2,1,0:T(8,128)(2,1)S(1)} collective-permute-done((bf16[1,144,128]{2,1,0:T(8,128)(2,1)}, bf16[1,144,128]{2,1,0:T(8,128)(2,1)S(1)}, u32[]{:S(2)}, u32[]{:S(2)}) %collective-permute-start.1) | collective-permute-done | bytes 36896 | tf_op jit(solution)/shard_map/ppermute | solution.py:70
  14.4 1.1 %collective-permute-start.2 = (bf16[1,144,128]{2,1,0:T(8,128)(2,1)}, bf16[1,144,128]{2,1,0:T(8,128)(2,1)S(1)}, u32[]{:S(2)}, u32[]{:S(2)}) collective-permute-start(bf16[1,144,128]{2,1,0:T(8,128)(2,1)} %bitcast.12), channel_id=1, source_target_pairs={{0,12},{4,8},{8,4},{12,0},{16,28},{20,24},{24,20},{28,16},{1,13},{... | collective-permute-start | bytes 110600 | tf_op jit(solution)/shard_map/ppermute | solution.py:70
  15.5 3.1 %collective-permute-done.2 = bf16[1,144,128]{2,1,0:T(8,128)(2,1)S(1)} collective-permute-done((bf16[1,144,128]{2,1,0:T(8,128)(2,1)}, bf16[1,144,128]{2,1,0:T(8,128)(2,1)S(1)}, u32[]{:S(2)}, u32[]{:S(2)}) %collective-permute-start.2) | collective-permute-done | bytes 36896 | tf_op jit(solution)/shard_map/ppermute | solution.py:70
  18.6 0.0 collective-permute-done.3
  18.7 0.0 collective-permute-done.4
  18.7 0.0 collective-permute-done.5
  18.7 0.0 copy-start
  18.8 1.3 %collective-permute-start.7 = (bf16[8,144,128]{2,1,0:T(8,128)(2,1)S(1)}, bf16[8,144,128]{2,1,0:T(8,128)(2,1)S(1)}, u32[]{:S(2)}, u32[]{:S(2)}) collective-permute-start(bf16[8,144,128]{2,1,0:T(8,128)(2,1)S(1)} %constant_dynamic-update-slice_fusion.refs_0_), channel_id=1, source_target_pairs={{0,2},{1,3},{2,0},{3,1},{4,6},{5,7},{6,4},{7,5},{8,10},{9,11},{10,... | collective-permute-start | bytes 884744 | tf_op jit(solution)/shard_map/ppermute | solution.py:70
  20.0 4.9 %collective-permute-start.8 = (bf16[8,144,128]{2,1,0:T(8,128)(2,1)S(1)}, bf16[8,144,128]{2,1,0:T(8,128)(2,1)S(1)}, u32[]{:S(2)}, u32[]{:S(2)}) collective-permute-start(bf16[8,144,128]{2,1,0:T(8,128)(2,1)S(1)} %constant_dynamic-update-slice_fusion.refs_0_), channel_id=1, source_target_pairs={{0,1},{1,0},{2,3},{3,2},{4,5},{5,4},{6,7},{7,6},{8,9},{9,8},{10,11... | collective-permute-start | bytes 884744 | tf_op jit(solution)/shard_map/ppermute | solution.py:70
  24.9 4.2 %pair_lists.1 = (s32[4,384]{1,0:T(4,128)}, s32[4,384]{1,0:T(4,128)}) custom-call(s32[4]{0:T(128)} %bitcast.16, s32[4,2,256]{2,1,0:T(2,128)} %bitcast.15), custom_call_target="tpu_custom_call" | custom-call | flops 10485760 | bytes 16384 | tf_op jit(solution)/shard_map/pair_lists/pallas_call | solution.py:279
  29.1 1.0 %collective-permute-start.9 = (bf16[8,144,128]{2,1,0:T(8,128)(2,1)S(1)}, bf16[8,144,128]{2,1,0:T(8,128)(2,1)S(1)}, u32[]{:S(2)}, u32[]{:S(2)}) collective-permute-start(bf16[8,144,128]{2,1,0:T(8,128)(2,1)S(1)} %collective-permute-done.7.refs_2_), channel_id=1, source_target_pairs={{0,1},{1,0},{2,3},{3,2},{4,5},{5,4},{6,7},{7,6},{8,9},{9,8},{10,11... | collective-permute-start | bytes 884744 | tf_op jit(solution)/shard_map/ppermute | solution.py:70
  30.1 1.2 %collective-permute-done.9.refs_3_ = bf16[8,144,128]{2,1,0:T(8,128)(2,1)S(1)} collective-permute-done((bf16[8,144,128]{2,1,0:T(8,128)(2,1)S(1)}, bf16[8,144,128]{2,1,0:T(8,128)(2,1)S(1)}, u32[]{:S(2)}, u32[]{:S(2)}) %collective-permute-start.9) | collective-permute-done | bytes 294944 | tf_op jit(solution)/shard_map/ppermute | solution.py:70
  31.4 0.7 copy-done.3
  32.1 14.6 %serial_transforms.1 = (bf16[4,8,128,128]{3,2,1,0:T(8,128)(2,1)}, bf16[4,8,128,128]{3,2,1,0:T(8,128)(2,1)}, bf16[4,8,16,128]{3,2,1,0:T(8,128)(2,1)}) custom-call(bf16[8,144,128]{2,1,0:T(8,128)(2,1)} %copy-done, bf16[8,144,128]{2,1,0:T(8,128)(2,1)} %copy-done.2, bf16[8,144,128]{2,1,0:T(8,128)(2,1)} %copy-done.1, bf16[8,144,128]{2,1,0:T(8,128)(2,1)} %copy-done.3), custom_call_target="tpu_custom_call" | custom-call | tf_op jit(solution)/shard_map/serial_transforms/pallas_call | solution.py:218
  46.6 35.0 %cell_updates.1 = bf16[5120,128]{1,0:T(8,128)(2,1)} custom-call(s32[4,384]{1,0:T(4,128)} %get-tuple-element.21.entries, s32[4,384]{1,0:T(4,128)} %get-tuple-element.22.others, bf16[5120,128]{1,0:T(8,128)(2,1)} %state.1, bf16[3,5120]{1,0:T(4,128)(2,1)} %coord.1, bf16[4,8,128,128]{3,2,1,0:T(8,128)(2,1)} %get-tuple-element.24.bt, ...), custom_call_target="tpu_custom_call" | custom-call | tf_op jit(solution)/shard_map/cell_updates/pallas_call | solution.py:360
  (16 shorter events, 0.1 us)
Async XLA Ops:
  1.5 17.2 %collective-permute-start.6 = (bf16[1,144,128]{2,1,0:T(8,128)(2,1)}, bf16[1,144,128]{2,1,0:T(8,128)(2,1)S(1)}, u32[]{:S(2)}, u32[]{:S(2)}) collective-permute-start(bf16[1,144,128]{2,1,0:T(8,128)(2,1)} %bitcast.6), channel_id=1, source_target_pairs={{0,28},{4,24},{8,20},{12,16},{16,12},{20,8},{24,4},{28,0},{1,29},{... | collective-permute-start | bytes 110600 | tf_op jit(solution)/shard_map/ppermute | solution.py:70
  2.4 16.3 %collective-permute-start.5 = (bf16[1,144,128]{2,1,0:T(8,128)(2,1)}, bf16[1,144,128]{2,1,0:T(8,128)(2,1)S(1)}, u32[]{:S(2)}, u32[]{:S(2)}) collective-permute-start(bf16[1,144,128]{2,1,0:T(8,128)(2,1)} %bitcast.7), channel_id=1, source_target_pairs={{0,24},{4,28},{8,16},{12,20},{16,8},{20,12},{24,0},{28,4},{1,25},{... | collective-permute-start | bytes 110600 | tf_op jit(solution)/shard_map/ppermute | solution.py:70
  5.7 12.9 %collective-permute-start.4 = (bf16[1,144,128]{2,1,0:T(8,128)(2,1)}, bf16[1,144,128]{2,1,0:T(8,128)(2,1)S(1)}, u32[]{:S(2)}, u32[]{:S(2)}) collective-permute-start(bf16[1,144,128]{2,1,0:T(8,128)(2,1)} %bitcast.8), channel_id=1, source_target_pairs={{0,20},{4,16},{8,28},{12,24},{16,4},{20,0},{24,12},{28,8},{1,21},{... | collective-permute-start | bytes 110600 | tf_op jit(solution)/shard_map/ppermute | solution.py:70
  5.7 12.9 %collective-permute-start.3 = (bf16[1,144,128]{2,1,0:T(8,128)(2,1)}, bf16[1,144,128]{2,1,0:T(8,128)(2,1)S(1)}, u32[]{:S(2)}, u32[]{:S(2)}) collective-permute-start(bf16[1,144,128]{2,1,0:T(8,128)(2,1)} %bitcast.9), channel_id=1, source_target_pairs={{0,16},{4,20},{8,24},{12,28},{16,0},{20,4},{24,8},{28,12},{1,17},{... | collective-permute-start | bytes 110600 | tf_op jit(solution)/shard_map/ppermute | solution.py:70
  8.0 3.4 %collective-permute-start = (bf16[1,144,128]{2,1,0:T(8,128)(2,1)}, bf16[1,144,128]{2,1,0:T(8,128)(2,1)S(1)}, u32[]{:S(2)}, u32[]{:S(2)}) collective-permute-start(bf16[1,144,128]{2,1,0:T(8,128)(2,1)} %bitcast.10), channel_id=1, source_target_pairs={{0,4},{4,0},{8,12},{12,8},{16,20},{20,16},{24,28},{28,24},{1,5},{5... | collective-permute-start | bytes 110600 | tf_op jit(solution)/shard_map/ppermute | solution.py:70
  11.4 3.0 %collective-permute-start.1 = (bf16[1,144,128]{2,1,0:T(8,128)(2,1)}, bf16[1,144,128]{2,1,0:T(8,128)(2,1)S(1)}, u32[]{:S(2)}, u32[]{:S(2)}) collective-permute-start(bf16[1,144,128]{2,1,0:T(8,128)(2,1)} %bitcast.11), channel_id=1, source_target_pairs={{0,8},{4,12},{8,0},{12,4},{16,24},{20,28},{24,16},{28,20},{1,9},{5... | collective-permute-start | bytes 110600 | tf_op jit(solution)/shard_map/ppermute | solution.py:70
  14.4 4.2 %collective-permute-start.2 = (bf16[1,144,128]{2,1,0:T(8,128)(2,1)}, bf16[1,144,128]{2,1,0:T(8,128)(2,1)S(1)}, u32[]{:S(2)}, u32[]{:S(2)}) collective-permute-start(bf16[1,144,128]{2,1,0:T(8,128)(2,1)} %bitcast.12), channel_id=1, source_target_pairs={{0,12},{4,8},{8,4},{12,0},{16,28},{20,24},{24,20},{28,16},{1,13},{... | collective-permute-start | bytes 110600 | tf_op jit(solution)/shard_map/ppermute | solution.py:70
  18.7 12.6 %copy-start = (bf16[8,144,128]{2,1,0:T(8,128)(2,1)}, bf16[8,144,128]{2,1,0:T(8,128)(2,1)S(1)}, u32[]{:S(2)}) copy-start(bf16[8,144,128]{2,1,0:T(8,128)(2,1)S(1)} %constant_dynamic-update-slice_fusion.refs_0_) | copy-start | bytes 884740
  18.8 10.4 %collective-permute-start.7 = (bf16[8,144,128]{2,1,0:T(8,128)(2,1)S(1)}, bf16[8,144,128]{2,1,0:T(8,128)(2,1)S(1)}, u32[]{:S(2)}, u32[]{:S(2)}) collective-permute-start(bf16[8,144,128]{2,1,0:T(8,128)(2,1)S(1)} %constant_dynamic-update-slice_fusion.refs_0_), channel_id=1, source_target_pairs={{0,2},{1,3},{2,0},{3,1},{4,6},{5,7},{6,4},{7,5},{8,10},{9,11},{10,... | collective-permute-start | bytes 884744 | tf_op jit(solution)/shard_map/ppermute | solution.py:70
  20.0 10.1 %collective-permute-start.8 = (bf16[8,144,128]{2,1,0:T(8,128)(2,1)S(1)}, bf16[8,144,128]{2,1,0:T(8,128)(2,1)S(1)}, u32[]{:S(2)}, u32[]{:S(2)}) collective-permute-start(bf16[8,144,128]{2,1,0:T(8,128)(2,1)S(1)} %constant_dynamic-update-slice_fusion.refs_0_), channel_id=1, source_target_pairs={{0,1},{1,0},{2,3},{3,2},{4,5},{5,4},{6,7},{7,6},{8,9},{9,8},{10,11... | collective-permute-start | bytes 884744 | tf_op jit(solution)/shard_map/ppermute | solution.py:70
  29.1 2.2 %copy-start.1 = (bf16[8,144,128]{2,1,0:T(8,128)(2,1)}, bf16[8,144,128]{2,1,0:T(8,128)(2,1)S(1)}, u32[]{:S(2)}) copy-start(bf16[8,144,128]{2,1,0:T(8,128)(2,1)S(1)} %collective-permute-done.7.refs_2_) | copy-start | bytes 884740
  29.1 2.2 %collective-permute-start.9 = (bf16[8,144,128]{2,1,0:T(8,128)(2,1)S(1)}, bf16[8,144,128]{2,1,0:T(8,128)(2,1)S(1)}, u32[]{:S(2)}, u32[]{:S(2)}) collective-permute-start(bf16[8,144,128]{2,1,0:T(8,128)(2,1)S(1)} %collective-permute-done.7.refs_2_), channel_id=1, source_target_pairs={{0,1},{1,0},{2,3},{3,2},{4,5},{5,4},{6,7},{7,6},{8,9},{9,8},{10,11... | collective-permute-start | bytes 884744 | tf_op jit(solution)/shard_map/ppermute | solution.py:70
  30.1 1.2 %copy-start.2 = (bf16[8,144,128]{2,1,0:T(8,128)(2,1)}, bf16[8,144,128]{2,1,0:T(8,128)(2,1)S(1)}, u32[]{:S(2)}) copy-start(bf16[8,144,128]{2,1,0:T(8,128)(2,1)S(1)} %collective-permute-done.8.refs_1_) | copy-start | bytes 884740
  31.4 0.7 copy-start.3

commit v2 on v1

--- a/solution.py
+++ b/solution.py
@@ -16,7 +16,7 @@
 GROUP = 8
 F32 = jnp.float32
 BF16 = jnp.bfloat16
-VMEM_LIMIT = 56 * 1024 * 1024
+VMEM_LIMIT = 40 * 1024 * 1024
 
 
 def in_vmem():
@@ -39,9 +39,10 @@
 
 
 def mm_parts(a, b):
-    left = jnp.concatenate([a[0], a[0], a[1], a[0], a[1], a[2]], axis=1)
-    right = jnp.concatenate([b[0], b[1], b[0], b[2], b[1], b[0]], axis=0)
-    return mm16(left, right)
+    def two(i, j, m, n):
+        return mm16(jnp.concatenate([a[i], a[m]], axis=1), jnp.concatenate([b[j], b[n]], axis=0))
+
+    return two(0, 0, 0, 1) + (two(1, 0, 0, 2) + two(1, 1, 2, 0))
 
 
 def mm(a, b):
@@ -66,14 +67,24 @@
     )(pred, value, variance, coord)
 
 
+def steps_of(size):
+    return size.bit_length() - 1
+
+
+def place_of(mask, size):
+    steps = steps_of(size)
+    return sum(((mask >> (steps - 1 - s)) & 1) << s for s in range(steps))
+
+
 def swapped(block, axis, mask):
     return lax.ppermute(block, axis, [(i, i ^ mask) for i in range(lax.axis_size(axis))])
 
 
 def gathered(mine, meanwhile):
-    near = [mine[None]]
-    near += [swapped(near[0], "cell", mask) for mask in range(1, lax.axis_size("cell"))]
-    near, work = meanwhile(jnp.concatenate(near, axis=0))
+    near = mine[None]
+    for b in reversed(range(steps_of(lax.axis_size("cell")))):
+        near = jnp.concatenate([near, swapped(near, "cell", 1 << b)], axis=0)
+    near, work = meanwhile(near)
     pieces = {0: near}
     mask = lax.axis_size("dp") // 2
     while mask:
@@ -139,101 +150,6 @@
     scaled = parts(place * (2 * taper_rate * LOG2E))
     lines = [part[j : j + 1].astype(F32) for part in scaled for j in range(3)]
     return stacked(lines + ones + list(norm_parts(place))).astype(BF16)
-
-
-def chain_kernel(*refs):
-    pieces, (bt_out, mp_out, of_out, ys, wd, gs, us, both_ref) = refs[:-8], refs[-8:]
-    batches, tiles = bt_out.shape[:2]
-    members = bt_out.shape[2]
-    rows = lax.broadcasted_iota(jnp.int32, (members, members), 0)
-    cols = lax.broadcasted_iota(jnp.int32, (members, members), 1)
-    eye = jnp.where(rows == cols, 1.0, 0.0)
-    my_tile, my_batch = lax.axis_index("cell"), lax.axis_index("dp")
-
-    for rd in range(batches):
-        lefts, rights = [], []
-        k = my_batch ^ rd
-        for rc in range(tiles):
-            u = my_tile ^ rc
-            raw = pieces[rd][rc, :members, :]
-            y = raw.astype(F32)
-            e = pieces[rd][rc, members:, :].astype(F32)
-            value = e[0:1] + e[1:2] + e[2:3]
-            variance = e[3:4] + e[4:5] + e[5:6]
-            place = e[6:9]
-            mean = jnp.mean(y, axis=0, keepdims=True)
-            w = 1.0 / variance
-            where = pl.ds(pl.multiple_of(u * OBS_DEV, OBS_DEV), OBS_DEV)
-            ys[k, :, where] = raw
-            wd[k, 0:1, where] = w
-            wd[k, 1:2, where] = value
-            of_out[k, u] = obs_features(place)
-            z = jnp.broadcast_to((value - mean) * w, (16, OBS_DEV))
-            lefts.append(jnp.concatenate(parts(jnp.concatenate([(y - mean) * w, z], axis=0)), axis=0))
-            rights.append(raw)
-        g = lax.dot_general(
-            jnp.concatenate(lefts, axis=1), jnp.concatenate(rights, axis=1), (((1,), (1,)), ((), ())),
-            preferred_element_type=F32,
-        )
-        n = members + 16
-        g = g[:n] + g[n : 2 * n] + g[2 * n :]
-        g = g - jnp.mean(g, axis=1, keepdims=True)
-        gs[k] = g[:members]
-        us[k] = g[members:]
-
-    qt = eye - 1.0 / members
-    p = jnp.full((16, members), 1.0 / members, F32)
-    chunk = min(2, tiles) * OBS_DEV
-    for k in range(batches):
-        inverse = inverse_of(eye, gs[k] * (1.0 / (members - 1)), both_ref)
-        inverse_parts = parts(inverse)
-        qt_parts = parts(qt)
-        mt = mm_parts(inverse_parts, qt_parts)
-        ht = 0.5 * qt + p[0:1]
-        hi, mid, lo = parts(jnp.concatenate([mt, ht], axis=0))
-        twice = jnp.concatenate([hi, mid], axis=1)
-        for n in range(tiles * OBS_DEV // chunk):
-            where = pl.ds(n * chunk, chunk)
-            y = ys[k, :, where]
-            both = mm16(twice, jnp.concatenate([y, y], axis=0)) + mm16(lo, y)
-            b = (both[:members] * (1.0 / (members - 1))).astype(BF16)
-            pull = wd[k, 0:1, where] * (wd[k, 1:2, where] - both[members:])
-            for c in range(chunk // OBS_DEV):
-                u = n * (chunk // OBS_DEV) + c
-                bt_out[k, u] = b[:, c * OBS_DEV : (c + 1) * OBS_DEV]
-                mp_out[k, u] = pull[:, c * OBS_DEV : (c + 1) * OBS_DEV].T.astype(BF16)
-        if k + 1 < batches:
-            half = parts(0.5 * (eye + inverse))
-            step = parts(mm_parts(parts(us[k]), inverse_parts) * (1.0 / (members - 1)))
-            p = p + mm_parts(step, qt_parts)
-            qt = 0.5 * (qt + mt)
-            for j in range(k + 1, batches):
-                g_j = parts(gs[j])
-                gs[j] = mm_parts(half, parts(mm_parts(g_j, half)))
-                us[j] = mm_parts(parts(us[j] - mm_parts(step, g_j)), half)
-
-
-def chain(pieces, tiles, batches):
-    members = pieces[0].shape[1] - EXTRA
-    return pl.pallas_call(
-        chain_kernel,
-        out_shape=(
-            jax.ShapeDtypeStruct((batches, tiles, members, OBS_DEV), BF16),
-            jax.ShapeDtypeStruct((batches, tiles, OBS_DEV, members), BF16),
-            jax.ShapeDtypeStruct((batches, tiles, 16, OBS_DEV), BF16),
-        ),
-        in_specs=[in_vmem()] * len(pieces),
-        out_specs=(in_vmem(),) * 3,
-        scratch_shapes=[
-            pltpu.VMEM((batches, members, tiles * OBS_DEV), BF16),
-            pltpu.VMEM((batches, 8, tiles * OBS_DEV), F32),
-            pltpu.VMEM((batches, members, members), F32),
-            pltpu.VMEM((batches, 16, members), F32),
-            pltpu.VMEM((2 * members, members), F32),
-        ],
-        compiler_params=pltpu.CompilerParams(vmem_limit_bytes=VMEM_LIMIT),
-        name="serial_transforms",
-    )(*pieces)
 
 
 def list_kernel(sizes_in, pairs, entries, others, *, tiles, obs_tiles):
@@ -286,12 +202,28 @@
     )(counts, pairs)
 
 
-def cell_kernel(entries, others, state, coord, bt, mp, of, out, acc, pert, feat, held, tall):
-    batches, obs_tiles = bt.shape[:2]
+def filter_kernel(entries, others, coord, state, *refs, pieces_count):
+    pieces, out, scratch = refs[:pieces_count], refs[pieces_count], refs[pieces_count + 1 :]
+    blocks, ys, wd, of, gs, us, both_ref, bt, mp, prior, acc, pert, feat, held, tall, final, arrived, left = scratch
+    batches, obs_tiles = of.shape[:2]
     members = state.shape[1]
     tiles = state.shape[0] // CT
     several = 4 if tiles % 4 == 0 else 1
+
+    copies = [pltpu.make_async_copy(piece, blocks.at[d], arrived.at[d]) for d, piece in enumerate(pieces)]
+    copies.append(pltpu.make_async_copy(state, prior, arrived.at[pieces_count]))
+    for copy in copies:
+        copy.start()
+
+    rows = lax.broadcasted_iota(jnp.int32, (members, members), 0)
+    cols = lax.broadcasted_iota(jnp.int32, (members, members), 1)
+    eye = jnp.where(rows == cols, 1.0, 0.0)
+    my_tile, my_batch = lax.axis_index("cell"), lax.axis_index("dp")
+
     tall[...] = cell_features(coord[...].astype(F32))
+    acc[tiles] = jnp.zeros((CT, 2 * members), F32)
+    pert[tiles] = jnp.zeros((CT, members), BF16)
+    feat[tiles] = jnp.zeros((CT, 16), BF16)
 
     def over_tiles(body):
         def some(i, _):
@@ -301,21 +233,87 @@
 
         lax.fori_loop(0, tiles // several, some, 0)
 
+    def describe(t):
+        feat[t] = tall[:, pl.ds(pl.multiple_of(t * CT, CT), CT)].T.astype(BF16)
+
+    over_tiles(describe)
+
+    for rd in range(batches):
+        copies[rd].wait()
+        lefts, rights = [], []
+        k = my_batch ^ rd
+        for rc in range(obs_tiles):
+            u = my_tile ^ rc
+            r = place_of(rc, obs_tiles)
+            raw = blocks[rd, r, :members, :]
+            y = raw.astype(F32)
+            e = blocks[rd, r, members:, :].astype(F32)
+            value = e[0:1] + e[1:2] + e[2:3]
+            variance = e[3:4] + e[4:5] + e[5:6]
+            mean = jnp.mean(y, axis=0, keepdims=True)
+            w = 1.0 / variance
+            where = pl.ds(pl.multiple_of(u * OBS_DEV, OBS_DEV), OBS_DEV)
+            ys[k, :, where] = raw
+            wd[k, 0:1, where] = w
+            wd[k, 1:2, where] = value
+            of[k, u] = obs_features(e[6:9])
+            z = jnp.broadcast_to((value - mean) * w, (16, OBS_DEV))
+            lefts.append(parts(jnp.concatenate([(y - mean) * w, z], axis=0)))
+            rights.append(raw)
+        right = jnp.concatenate(rights, axis=1)
+        g = sum(
+            lax.dot_general(
+                jnp.concatenate(part, axis=1), right, (((1,), (1,)), ((), ())), preferred_element_type=F32
+            )
+            for part in zip(*lefts)
+        )
+        g = g - jnp.mean(g, axis=1, keepdims=True)
+        gs[k] = g[:members]
+        us[k] = g[members:]
+
+    copies[pieces_count].wait()
+
     def prepare(t):
-        where = pl.ds(pl.multiple_of(t * CT, CT), CT)
-        acc[t] = state[where, :].astype(F32)
-        feat[t] = tall[:, where].T.astype(BF16)
+        x = prior[pl.ds(pl.multiple_of(t * CT, CT), CT), :].astype(F32)
+        acc[t, :, :members] = x
+        acc[t, :, members:] = x - jnp.mean(x, axis=1, keepdims=True)
 
     over_tiles(prepare)
-    acc[tiles] = jnp.zeros((CT, members), F32)
-    pert[tiles] = jnp.zeros((CT, members), BF16)
-    feat[tiles] = jnp.zeros((CT, 16), BF16)
-
+
+    qt = eye - 1.0 / members
+    p = jnp.full((16, members), 1.0 / members, F32)
+    chunk = min(2, obs_tiles) * OBS_DEV
     for k in range(batches):
+        inverse = inverse_of(eye, gs[k] * (1.0 / (members - 1)), both_ref)
+        inverse_parts = parts(inverse)
+        qt_parts = parts(qt)
+        mt = mm_parts(inverse_parts, qt_parts)
+        ht = 0.5 * qt + p[0:1]
+        hi, mid, lo = parts(jnp.concatenate([mt, ht], axis=0))
+        twice = jnp.concatenate([hi, mid], axis=1)
+        for n in range(obs_tiles * OBS_DEV // chunk):
+            where = pl.ds(n * chunk, chunk)
+            y = ys[k, :, where]
+            both = mm16(twice, jnp.concatenate([y, y], axis=0)) + mm16(lo, y)
+            b = (both[:members] * (1.0 / (members - 1))).astype(BF16)
+            pull = wd[k, 0:1, where] * (wd[k, 1:2, where] - both[members:])
+            pulls = jnp.concatenate([pull, pull - jnp.mean(pull, axis=0, keepdims=True)], axis=0).astype(BF16)
+            for c in range(chunk // OBS_DEV):
+                u = n * (chunk // OBS_DEV) + c
+                bt[u] = b[:, c * OBS_DEV : (c + 1) * OBS_DEV]
+                mp[u] = pulls[:, c * OBS_DEV : (c + 1) * OBS_DEV].T
+        if k + 1 < batches:
+            half = parts(0.5 * (eye + inverse))
+            step = parts(mm_parts(parts(us[k]), inverse_parts) * (1.0 / (members - 1)))
+            p = p + mm_parts(step, qt_parts)
+            qt = 0.5 * (qt + mt)
+            for j in range(k + 1, batches):
+                g_j = parts(gs[j])
+                gs[j] = mm_parts(half, parts(mm_parts(g_j, half)))
+                us[j] = mm_parts(parts(us[j] - mm_parts(step, g_j)), half)
 
         def centre(t):
-            x = acc[t]
-            pert[t] = ((x - jnp.mean(x, axis=1, keepdims=True))).astype(BF16)
+            pert[t] = acc[t, :, members:].astype(BF16)
 
         over_tiles(centre)
 
@@ -326,52 +324,80 @@
         def weigh(i):
             for j in range(GROUP):
                 t, u0, u1, m0, m1 = named(i, j)
-                score = mm16(pert[t], jnp.concatenate([bt[k, u0], bt[k, u1]], axis=1))
+                score = mm16(pert[t], jnp.concatenate([bt[u0], bt[u1]], axis=1))
                 power = mm16(feat[t], jnp.concatenate([of[k, u0], of[k, u1]], axis=1))
                 taper = jnp.exp2(power)
                 for n, m in enumerate((m0, m1)):
                     cut = slice(n * OBS_DEV, (n + 1) * OBS_DEV)
                     held[j, :, cut] = (taper[:, cut] * (score[:, cut] * m.astype(F32))).astype(BF16)
 
-        def pull(i):
+        def draw(i):
             for j in range(GROUP):
                 t, u0, u1, _, _ = named(i, j)
-                acc[t] += mm16(held[j], jnp.concatenate([mp[k, u0], mp[k, u1]], axis=0))
+                acc[t] += mm16(held[j], jnp.concatenate([mp[u0], mp[u1]], axis=0))
 
         def group(i, _):
-            pull(i - 1)
+            draw(i - 1)
             weigh(i)
             return 0
 
         groups = (others[k, others.shape[1] - 1] + GROUP - 1) // GROUP
         weigh(0)
         lax.fori_loop(1, groups, group, 0)
-        pull(groups - 1)
-
-    def finish(t):
-        out[pl.ds(pl.multiple_of(t * CT, CT), CT), :] = acc[t].astype(BF16)
-
-    over_tiles(finish)
-
-
-def cells(entries, others, state, coord, bt, mp, of):
+        draw(groups - 1)
+
+    leaving = []
+    for n in range(left.shape[0]):
+        share = tiles // left.shape[0]
+
+        def finish(i, _):
+            t = n * share + i
+            final[pl.ds(pl.multiple_of(t * CT, CT), CT), :] = acc[t, :, :members].astype(BF16)
+            return 0
+
+        lax.fori_loop(0, share, finish, 0)
+        where = pl.ds(n * share * CT, share * CT)
+        leaving.append(pltpu.make_async_copy(final.at[where], out.at[where], left.at[n]))
+        leaving[-1].start()
+    for copy in leaving:
+        copy.wait()
+
+
+def filtered(entries, others, coord, state, pieces):
+    batches = len(pieces)
+    obs_tiles, rows = pieces[0].shape[:2]
     members = state.shape[1]
     tiles = state.shape[0] // CT
+    shares = 4 if tiles % 4 == 0 else 1
+    anywhere = pl.BlockSpec(memory_space=pl.ANY)
     return pl.pallas_call(
-        cell_kernel,
+        functools.partial(filter_kernel, pieces_count=batches),
         out_shape=jax.ShapeDtypeStruct(state.shape, BF16),
-        in_specs=[in_smem()] * 2 + [in_vmem()] * 5,
-        out_specs=in_vmem(),
+        in_specs=[in_smem()] * 2 + [in_vmem()] + [anywhere] * (1 + batches),
+        out_specs=anywhere,
         scratch_shapes=[
-            pltpu.VMEM((tiles + 1, CT, members), F32),
+            pltpu.VMEM((batches, obs_tiles, rows, OBS_DEV), BF16),
+            pltpu.VMEM((batches, members, obs_tiles * OBS_DEV), BF16),
+            pltpu.VMEM((batches, 8, obs_tiles * OBS_DEV), F32),
+            pltpu.VMEM((batches, obs_tiles, 16, OBS_DEV), BF16),
+            pltpu.VMEM((batches, members, members), F32),
+            pltpu.VMEM((batches, 16, members), F32),
+            pltpu.VMEM((2 * members, members), F32),
+            pltpu.VMEM((obs_tiles, members, OBS_DEV), BF16),
+            pltpu.VMEM((obs_tiles, OBS_DEV, 2 * members), BF16),
+            pltpu.VMEM(state.shape, BF16),
+            pltpu.VMEM((tiles + 1, CT, 2 * members), F32),
             pltpu.VMEM((tiles + 1, CT, members), BF16),
             pltpu.VMEM((tiles + 1, CT, 16), BF16),
             pltpu.VMEM((GROUP, CT, 2 * OBS_DEV), BF16),
             pltpu.VMEM((16, tiles * CT), F32),
+            pltpu.VMEM(state.shape, BF16),
+            pltpu.SemaphoreType.DMA((batches + 1,)),
+            pltpu.SemaphoreType.DMA((shares,)),
         ],
         compiler_params=pltpu.CompilerParams(vmem_limit_bytes=VMEM_LIMIT),
-        name="cell_updates",
-    )(entries, others, state, coord, bt, mp, of)
+        name="filter",
+    )(entries, others, coord, state, *pieces)
 
 
 def local(
@@ -394,8 +420,7 @@
         return near, pair_lists(pairs, counts, tiles, obs_tiles)
 
     pieces, (entries, others) = gathered(mine, meanwhile)
-    bt, mp, of = chain(pieces, obs_tiles, batches)
-    return cells(entries, others, state, cell_coordinate, bt, mp, of)
+    return filtered(entries, others, cell_coordinate, state, pieces)
 
 
 def solution(mesh):

time: 80.9 us -> 76.5 us (0.946)
  the two profiles are of different devices: /device:TPU:25 before, /device:TPU:8 now
where the time goes in v2:
time: 76.5 us; the launch traced here: 75 us
  Pallas kernels  50.2 us (66%)
  waiting for transfers between devices  12.5 us (16%)
  starting transfers between devices  6.25 us (8%)
  local copies, waits for them, and re-layouts  3.48 us (5%)
  other arithmetic  2.36 us (3%)
    pallas_call x1, Pallas kernels, filtered(): pl.pallas_call(functools.partial(filter_kernel, pieces_count=batches), ou...  44.5 us
    ppermute x6, waiting for transfers between devices, swapped(): lax.ppermute(block, axis, [(i, i ^ mask) for i in range(lax.axis_size(axi...  12.5 us
    ppermute x6, starting transfers between devices, swapped(): lax.ppermute(block, axis, [(i, i ^ mask) for i in range(lax.axis_size(axi...  6.25 us
    pallas_call x1, Pallas kernels, pair_lists(): pl.pallas_call(functools.partial(list_kernel, tiles=tiles, obs_tiles=obs_...  4.22 us
    unnamed x8, local copies, waits for them, and re-layouts  3.48 us
    concatenate x3, other arithmetic, gathered(): near = jnp.concatenate([near, swapped(near, 'cell', 1 << b)], axis=0)  2.36 us
  transfers between devices with their start and end apart: 6, of which 5 were waited for; matrix products, arithmetic and copies ran while one was open for 0% of the time, Pallas kernels for 6%

profile of v2, /device:TPU:8, one launch (start us, length us, event | category | flops | bytes accessed | tf_op | source)
XLA Modules:
  0.0 75.0 jit_solution(8212860076085310577)
XLA Ops:
  0.0 1.5 %pack_observations.1 = bf16[144,128]{1,0:T(8,128)(2,1)} custom-call(bf16[128,128]{1,0:T(8,128)(2,1)} %bitcast.9, f32[1,128]{1,0:T(1,128)} %value.1, f32[1,128]{1,0:T(1,128)} %variance.1, bf16[3,128]{1,0:T(4,128)(2,1)} %bitcast.10), custom_call_target="tpu_custom_call" | custom-call | tf_op jit(solution)/shard_map/pack_observations/pallas_call | solution.py:61
  1.5 2.6 %collective-permute-start = (bf16[1,144,128]{2,1,0:T(8,128)(2,1)}, bf16[1,144,128]{2,1,0:T(8,128)(2,1)S(1)}, u32[]{:S(2)}, u32[]{:S(2)}) collective-permute-start(bf16[1,144,128]{2,1,0:T(8,128)(2,1)} %bitcast.5), channel_id=1, source_target_pairs={{0,16},{4,20},{8,24},{12,28},{16,0},{20,4},{24,8},{28,12},{1,17},{... | collective-permute-start | bytes 110600 | tf_op jit(solution)/shard_map/ppermute | solution.py:80
  4.1 2.5 %collective-permute-done = bf16[1,144,128]{2,1,0:T(8,128)(2,1)S(1)} collective-permute-done((bf16[1,144,128]{2,1,0:T(8,128)(2,1)}, bf16[1,144,128]{2,1,0:T(8,128)(2,1)S(1)}, u32[]{:S(2)}, u32[]{:S(2)}) %collective-permute-start) | collective-permute-done | bytes 36896 | tf_op jit(solution)/shard_map/ppermute | solution.py:80
  6.6 0.8 %pad_maximum_fusion.2 = bf16[2,144,128]{2,1,0:T(8,128)(2,1)S(1)} fusion(bf16[1,144,128]{2,1,0:T(8,128)(2,1)S(1)} %collective-permute-done, bf16[1,144,128]{2,1,0:T(8,128)(2,1)} %bitcast.6), kind=kLoop, calls=%fused_computation.2 | loop fusion | flops 36864 | bytes 147456 | tf_op jit(solution)/shard_map/concatenate | solution.py:86
  7.3 0.5 collective-permute-start.1
  7.9 3.8 %collective-permute-done.1 = bf16[2,144,128]{2,1,0:T(8,128)(2,1)S(1)} collective-permute-done((bf16[2,144,128]{2,1,0:T(8,128)(2,1)S(1)}, bf16[2,144,128]{2,1,0:T(8,128)(2,1)S(1)}, u32[]{:S(2)}, u32[]{:S(2)}) %collective-permute-start.1) | collective-permute-done | bytes 73760 | tf_op jit(solution)/shard_map/ppermute | solution.py:80
  11.7 0.8 %pad_maximum_fusion.1 = bf16[4,144,128]{2,1,0:T(8,128)(2,1)S(1)} fusion(bf16[2,144,128]{2,1,0:T(8,128)(2,1)S(1)} %collective-permute-done.1, bf16[1,144,128]{2,1,0:T(8,128)(2,1)S(1)} %collective-permute-done, bf16[1,144,128]{2,1,0:T(8,128)(2,1)} %bitcast.7), kind=kLoop, calls=%fused_computation.1 | loop fusion | flops 147456 | bytes 294912 | tf_op jit(solution)/shard_map/concatenate | solution.py:86
  12.5 1.6 %collective-permute-start.2 = (bf16[4,144,128]{2,1,0:T(8,128)(2,1)S(1)}, bf16[4,144,128]{2,1,0:T(8,128)(2,1)S(1)}, u32[]{:S(2)}, u32[]{:S(2)}) collective-permute-start(bf16[4,144,128]{2,1,0:T(8,128)(2,1)S(1)} %pad_maximum_fusion.1), channel_id=1, source_target_pairs={{0,4},{4,0},{8,12},{12,8},{16,20},{20,16},{24,28},{28,24},{1,5},{5... | collective-permute-start | bytes 442376 | tf_op jit(solution)/shard_map/ppermute | solution.py:80
  14.1 3.6 %collective-permute-done.2 = bf16[4,144,128]{2,1,0:T(8,128)(2,1)S(1)} collective-permute-done((bf16[4,144,128]{2,1,0:T(8,128)(2,1)S(1)}, bf16[4,144,128]{2,1,0:T(8,128)(2,1)S(1)}, u32[]{:S(2)}, u32[]{:S(2)}) %collective-permute-start.2) | collective-permute-done | bytes 147488 | tf_op jit(solution)/shard_map/ppermute | solution.py:80
  17.7 0.8 %pad_maximum_fusion.refs_0_ = bf16[8,144,128]{2,1,0:T(8,128)(2,1)S(1)} fusion(bf16[4,144,128]{2,1,0:T(8,128)(2,1)S(1)} %collective-permute-done.2, bf16[2,144,128]{2,1,0:T(8,128)(2,1)S(1)} %collective-permute-done.1, bf16[1,144,128]{2,1,0:T(8,128)(2,1)S(1)} %collective-permute-done, bf16[1,144,128]{2,1,0:T(8,128)(2,1)} %bitcast.8), kind=kLoop, calls=%fused_computation | loop fusion | flops 442368 | bytes 589824 | tf_op jit(solution)/shard_map/concatenate | solution.py:86
  18.5 1.6 %collective-permute-start.3 = (bf16[8,144,128]{2,1,0:T(8,128)(2,1)S(1)}, bf16[8,144,128]{2,1,0:T(8,128)(2,1)S(1)}, u32[]{:S(2)}, u32[]{:S(2)}) collective-permute-start(bf16[8,144,128]{2,1,0:T(8,128)(2,1)S(1)} %pad_maximum_fusion.refs_0_), channel_id=1, source_target_pairs={{0,2},{1,3},{2,0},{3,1},{4,6},{5,7},{6,4},{7,5},{8,10},{9,11},{10,... | collective-permute-start | bytes 884744 | tf_op jit(solution)/shard_map/ppermute | solution.py:80
  20.0 0.0 collective-permute-start.4
  20.1 4.2 %pair_lists.1 = (s32[4,384]{1,0:T(4,128)}, s32[4,384]{1,0:T(4,128)}) custom-call(s32[4]{0:T(128)} %bitcast.12, s32[4,2,256]{2,1,0:T(2,128)} %bitcast.11), custom_call_target="tpu_custom_call" | custom-call | flops 10485760 | bytes 16384 | tf_op jit(solution)/shard_map/pair_lists/pallas_call | solution.py:195
  24.3 1.0 %collective-permute-done.3.refs_2_ = bf16[8,144,128]{2,1,0:T(8,128)(2,1)S(1)} collective-permute-done((bf16[8,144,128]{2,1,0:T(8,128)(2,1)S(1)}, bf16[8,144,128]{2,1,0:T(8,128)(2,1)S(1)}, u32[]{:S(2)}, u32[]{:S(2)}) %collective-permute-start.3) | collective-permute-done | bytes 294944 | tf_op jit(solution)/shard_map/ppermute | solution.py:80
  25.3 0.0 collective-permute-start.5
  25.3 0.0 collective-permute-done.4.refs_1_
  25.3 1.6 %collective-permute-done.5.refs_3_ = bf16[8,144,128]{2,1,0:T(8,128)(2,1)S(1)} collective-permute-done((bf16[8,144,128]{2,1,0:T(8,128)(2,1)S(1)}, bf16[8,144,128]{2,1,0:T(8,128)(2,1)S(1)}, u32[]{:S(2)}, u32[]{:S(2)}) %collective-permute-start.5) | collective-permute-done | bytes 294944 | tf_op jit(solution)/shard_map/ppermute | solution.py:80
  26.9 0.0 copy-start
  26.9 1.3 %copy-done = bf16[5120,128]{1,0:T(8,128)(2,1)S(1)} copy-done((bf16[5120,128]{1,0:T(8,128)(2,1)S(1)}, bf16[5120,128]{1,0:T(8,128)(2,1)}, u32[]{:S(2)}) %copy-start) | copy-done | bytes 1310744
  28.2 0.0 copy-start.1
  28.2 0.8 %copy-done.1 = bf16[3,5120]{1,0:T(4,128)(2,1)S(1)} copy-done((bf16[3,5120]{1,0:T(4,128)(2,1)S(1)}, bf16[3,5120]{1,0:T(4,128)(2,1)}, u32[]{:S(2)}) %copy-start.1) | copy-done | bytes 30744
  29.0 0.7 copy-done.2
  29.7 0.7 copy-done.3
  30.3 44.5 %filter.1 = bf16[5120,128]{1,0:T(8,128)(2,1)} custom-call(s32[4,384]{1,0:T(4,128)S(1)} %copy-done.2, s32[4,384]{1,0:T(4,128)S(1)} %copy-done.3, bf16[3,5120]{1,0:T(4,128)(2,1)S(1)} %copy-done.1, bf16[5120,128]{1,0:T(8,128)(2,1)S(1)} %copy-done, bf16[8,144,128]{2,1,0:T(8,128)(2,1)S(1)} %pad_maximum_fusion.refs_0_, ...), custom_call_target="tpu_custom_call" | custom-call | tf_op jit(solution)/shard_map/filter/pallas_call | solution.py:373
  (2 shorter events, 0.0 us)
Async XLA Ops:
  1.5 5.1 %collective-permute-start = (bf16[1,144,128]{2,1,0:T(8,128)(2,1)}, bf16[1,144,128]{2,1,0:T(8,128)(2,1)S(1)}, u32[]{:S(2)}, u32[]{:S(2)}) collective-permute-start(bf16[1,144,128]{2,1,0:T(8,128)(2,1)} %bitcast.5), channel_id=1, source_target_pairs={{0,16},{4,20},{8,24},{12,28},{16,0},{20,4},{24,8},{28,12},{1,17},{... | collective-permute-start | bytes 110600 | tf_op jit(solution)/shard_map/ppermute | solution.py:80
  7.3 4.4 %collective-permute-start.1 = (bf16[2,144,128]{2,1,0:T(8,128)(2,1)S(1)}, bf16[2,144,128]{2,1,0:T(8,128)(2,1)S(1)}, u32[]{:S(2)}, u32[]{:S(2)}) collective-permute-start(bf16[2,144,128]{2,1,0:T(8,128)(2,1)S(1)} %pad_maximum_fusion.2), channel_id=1, source_target_pairs={{0,8},{4,12},{8,0},{12,4},{16,24},{20,28},{24,16},{28,20},{1,9},{5... | collective-permute-start | bytes 221192 | tf_op jit(solution)/shard_map/ppermute | solution.py:80
  12.5 5.2 %collective-permute-start.2 = (bf16[4,144,128]{2,1,0:T(8,128)(2,1)S(1)}, bf16[4,144,128]{2,1,0:T(8,128)(2,1)S(1)}, u32[]{:S(2)}, u32[]{:S(2)}) collective-permute-start(bf16[4,144,128]{2,1,0:T(8,128)(2,1)S(1)} %pad_maximum_fusion.1), channel_id=1, source_target_pairs={{0,4},{4,0},{8,12},{12,8},{16,20},{20,16},{24,28},{28,24},{1,5},{5... | collective-permute-start | bytes 442376 | tf_op jit(solution)/shard_map/ppermute | solution.py:80
  18.5 6.8 %collective-permute-start.3 = (bf16[8,144,128]{2,1,0:T(8,128)(2,1)S(1)}, bf16[8,144,128]{2,1,0:T(8,128)(2,1)S(1)}, u32[]{:S(2)}, u32[]{:S(2)}) collective-permute-start(bf16[8,144,128]{2,1,0:T(8,128)(2,1)S(1)} %pad_maximum_fusion.refs_0_), channel_id=1, source_target_pairs={{0,2},{1,3},{2,0},{3,1},{4,6},{5,7},{6,4},{7,5},{8,10},{9,11},{10,... | collective-permute-start | bytes 884744 | tf_op jit(solution)/shard_map/ppermute | solution.py:80
  20.0 5.2 %collective-permute-start.4 = (bf16[8,144,128]{2,1,0:T(8,128)(2,1)S(1)}, bf16[8,144,128]{2,1,0:T(8,128)(2,1)S(1)}, u32[]{:S(2)}, u32[]{:S(2)}) collective-permute-start(bf16[8,144,128]{2,1,0:T(8,128)(2,1)S(1)} %pad_maximum_fusion.refs_0_), channel_id=1, source_target_pairs={{0,1},{1,0},{2,3},{3,2},{4,5},{5,4},{6,7},{7,6},{8,9},{9,8},{10,11... | collective-permute-start | bytes 884744 | tf_op jit(solution)/shard_map/ppermute | solution.py:80
  25.3 1.6 %collective-permute-start.5 = (bf16[8,144,128]{2,1,0:T(8,128)(2,1)S(1)}, bf16[8,144,128]{2,1,0:T(8,128)(2,1)S(1)}, u32[]{:S(2)}, u32[]{:S(2)}) collective-permute-start(bf16[8,144,128]{2,1,0:T(8,128)(2,1)S(1)} %collective-permute-done.3.refs_2_), channel_id=1, source_target_pairs={{0,1},{1,0},{2,3},{3,2},{4,5},{5,4},{6,7},{7,6},{8,9},{9,8},{10,11... | collective-permute-start | bytes 884744 | tf_op jit(solution)/shard_map/ppermute | solution.py:80
  26.9 1.3 %copy-start = (bf16[5120,128]{1,0:T(8,128)(2,1)S(1)}, bf16[5120,128]{1,0:T(8,128)(2,1)}, u32[]{:S(2)}) copy-start(bf16[5120,128]{1,0:T(8,128)(2,1)} %state.1) | copy-start | bytes 3932164
  28.2 0.8 %copy-start.1 = (bf16[3,5120]{1,0:T(4,128)(2,1)S(1)}, bf16[3,5120]{1,0:T(4,128)(2,1)}, u32[]{:S(2)}) copy-start(bf16[3,5120]{1,0:T(4,128)(2,1)} %coord.1) | copy-start | bytes 92164
  29.0 0.7 copy-start.2
  29.7 0.7 copy-start.3
